TPU v7x, 256 devices: a whole 4x4x8 slice. The times are simulated.
256 devices in a mesh: tile: 32 (over x, z), depth: 8 (over y, core).
Axes of the slice: x: 4, y: 4, z: 8, core: 2. Of those that a mesh axis runs over, the one named last changes fastest.
Arguments:
- perturbation: float32 [4, 32, 1024, 128], P(None, 'depth', 'tile'), may hold values from -6 to 6
- cotangent: float32 [4, 32, 1024, 128], P(None, 'depth', 'tile'), may hold values from -6 to 6
- land_mask: int32 [1024, 128], P('tile'), may hold values 0 or 1
- bottom_level: int32 [1024, 128], P('tile'), may hold values from 1 to 32
- mix_gain: float32 [32, 1024, 128], P('depth', 'tile'), may hold values from 0.5 to 1.5
- expansion: float32 [32, 1024, 128], P('depth', 'tile'), may hold values from 0.1 to 1
- contraction: float32 [32, 1024, 128], P('depth', 'tile'), may hold values from 0.1 to 1
- columns: int32 [131072], P('tile'), may hold values from 0 to 4095
- owners: int32 [131072, 1], P('tile'), may hold values from 0 to 31; in each aligned block of 4096 rows (0 to 4095, 4096 to 8191, ...) at most 256 rows name the same one
- level_start: int32 [131072], P('tile'), may hold values from 0 to 15
- level_count: int32 [131072], P('tile'), may hold values from 1 to 16
Outputs:
- final_state: float32 [4, 32, 1024, 128], P(None, 'depth', 'tile')
- adjoint_state: float32 [4, 32, 1024, 128], P(None, 'depth', 'tile')
- profiles: float32 [4, 32, 32, 8192], P(None, 'depth', 'tile')
- sensitivity: float32 [32, 8192], P('tile')
Inputs may be any that keep to these rules, and one draw needn't show every extreme that they name: `owners`: among the 4096 candidates listed by one tile, no owner is named more than 256 times; some owner is named exactly 256 times by some tile.
All inputs are finite; a program needn't handle non-finite values. No bound on the sum of `land_mask` on one device may be relied on, other than what follows from the above.
Results may differ from a plain program's by a relative error of at most 0.00002.
Values sent between devices are 32-bit elements; how exact they have to be, the bound alone decides.
A program may use at most 64 MiB of HBM per device.

v0:
```python
import math

import jax
import jax.numpy as jnp
from jax import lax
from jax.sharding import PartitionSpec as P

STEPS = 2


nu_horiz = 0.06
nu_vert = 0.08
press_coef = 0.1
grav_step = 0.2
sens_scale = 0.2


def padded_2(x, sides, width):
    for axis, dim in sides:
        devices, length = (lax.axis_size(axis), x.shape[dim])
        up = [(i, (i + 1) % devices) for i in range(devices - 1)]
        down = [(j, i) for i, j in up]
        last = lax.slice_in_dim(x, length - width, length, axis=dim)
        first = lax.slice_in_dim(x, 0, width, axis=dim)
        before = lax.ppermute(last, axis, up)
        after = lax.ppermute(first, axis, down)
        x = jnp.concatenate([before, x, after], axis=dim)
    return x


def prefix(x, axis, combine, identity, reverse):
    devices, place = (lax.axis_size(axis), lax.axis_index(axis))
    everything = lax.all_gather(x, axis)
    start = jnp.broadcast_to(jnp.asarray(identity, x.dtype), x.shape)

    def lap(k, before):
        at = devices - 1 - k if reverse else k
        reached = at > place if reverse else at < place
        new = combine(before, everything[at])
        return jnp.where(reached, new, before)

    return lax.fori_loop(0, devices, lap, start)


def spread(padded):
    center = padded[:, 1:-1, 1:-1]
    horizontal = (
        padded[:, 1:-1, 2:]
        + padded[:, 1:-1, :-2]
        + jnp.roll(center, 1, 3)
        + jnp.roll(center, -1, 3)
        - 4.0 * center
    )
    vertical = padded[:, 2:, 1:-1] + padded[:, :-2, 1:-1] - 2.0 * center
    return nu_horiz * horizontal + nu_vert * vertical


def east_diff(field):
    return 0.5 * (jnp.roll(field, -1, 2) - jnp.roll(field, 1, 2))


def north_diff(padded_field):
    return 0.5 * (padded_field[1:-1, 2:] - padded_field[1:-1, :-2])


def rotation(row_ids, total_rows):
    return 0.4 * jnp.sin(math.pi * ((row_ids.astype(jnp.float32) + 0.5) / total_rows - 0.5))


def rim_cells(stacked):
    return padded_2(stacked, (("tile", 2), ("depth", 1)), 1)


def column_sum(values, reverse):
    if reverse:
        running = jnp.flip(jnp.cumsum(jnp.flip(values, 0), 0), 0)
        column_total = running[0]
    else:
        running = jnp.cumsum(values, 0)
        column_total = running[-1]
    earlier_sum = prefix(
        column_total,
        "depth",
        lambda earlier, later: earlier + later,
        jnp.zeros_like(column_total),
        reverse,
    )
    return running + earlier_sum[None]


def forward_prepare(fields, coeffs):
    wet_mask, mix_gain, expansion, contraction, coriolis = coeffs
    pressure = grav_step * column_sum(contraction * fields[1] - expansion * fields[0], False)
    stacked = jnp.concatenate([wet_mask * mix_gain * fields, pressure[None]], 0)
    return (stacked, pressure)


def forward_finish(fields, padded, pressure, coeffs):
    wet_mask, mix_gain, expansion, contraction, coriolis = coeffs
    mixing = mix_gain * wet_mask * spread(padded[:4])
    new_temp = fields[0] + mixing[0]
    new_salt = fields[1] + mixing[1]
    new_east = fields[2] + mixing[2] + coriolis * fields[3] - press_coef * east_diff(pressure)
    new_north = fields[3] + mixing[3] - coriolis * fields[2] - press_coef * north_diff(padded[4])
    return wet_mask * jnp.stack([new_temp, new_salt, new_east, new_north], 0)


def backward_prepare(adjoint_in, coeffs):
    wet_mask, mix_gain, expansion, contraction, coriolis = coeffs
    masked = wet_mask * adjoint_in
    stacked = jnp.concatenate([wet_mask * mix_gain * masked, masked[3:4]], 0)
    return (masked, stacked)


def backward_finish(masked, padded, coeffs):
    wet_mask, mix_gain, expansion, contraction, coriolis = coeffs
    mixing = mix_gain * wet_mask * spread(padded[:4])
    pressure_bar = press_coef * (east_diff(masked[2]) + north_diff(padded[4]))
    density_bar = grav_step * column_sum(pressure_bar, True)
    out_temp = masked[0] + mixing[0] - expansion * density_bar
    out_salt = masked[1] + mixing[1] + contraction * density_bar
    out_east = masked[2] + mixing[2] - coriolis * masked[3]
    out_north = masked[3] + mixing[3] + coriolis * masked[2]
    return jnp.stack([out_temp, out_salt, out_east, out_north], 0)


def shards(
    perturbation,
    cotangent,
    land_mask,
    bottom_level,
    mix_gain,
    expansion,
    contraction,
    columns,
    owners,
    level_start,
    level_count,
):
    levels_here = perturbation.shape[1]
    rows_here = perturbation.shape[2]
    width = perturbation.shape[3]
    tile_count = lax.axis_size("tile")
    level_ids = lax.axis_index("depth") * levels_here + jnp.arange(levels_here, dtype=jnp.int32)
    wet_mask = ((land_mask[None] == 1) & (level_ids[:, None, None] < bottom_level[None])).astype(
        jnp.float32
    )
    row_ids = lax.axis_index("tile") * rows_here + jnp.arange(rows_here, dtype=jnp.int32)
    coriolis = rotation(row_ids, rows_here * tile_count)[None, :, None]
    coeffs = (wet_mask, mix_gain, expansion, contraction, coriolis)
    fields = perturbation
    adjoint_now = cotangent
    for repeat in range(STEPS):
        forward_stack, pressure = forward_prepare(fields, coeffs)
        fields = forward_finish(fields, rim_cells(forward_stack), pressure, coeffs)
    for repeat in range(STEPS):
        masked, backward_stack = backward_prepare(adjoint_now, coeffs)
        adjoint_now = backward_finish(masked, rim_cells(backward_stack), coeffs)
    cand_count = columns.shape[0]
    capacity = 2 * cand_count // tile_count
    owner_flat = owners[:, 0]
    onehot = (owner_flat[:, None] == jnp.arange(tile_count, dtype=jnp.int32)[None, :]).astype(
        jnp.int32
    )
    slot_rank = jnp.sum((jnp.cumsum(onehot, 0) - 1) * onehot, 1)
    slot_ids = owner_flat * capacity + slot_rank
    kept_mask = (
        (level_ids[:, None] >= level_start[None])
        & (level_ids[:, None] < (level_start + level_count)[None])
    ).astype(jnp.float32)
    picked = jnp.take(fields.reshape(4 * levels_here, rows_here * width), columns, axis=1)
    kept_vals = picked.reshape(4, levels_here, cand_count) * kept_mask[None]
    adjoint_picked = jnp.take(
        adjoint_now.reshape(4 * levels_here, rows_here * width), columns, axis=1
    )
    partial_value = sens_scale * jnp.sum(
        adjoint_picked.reshape(4, levels_here, cand_count) * kept_vals, (0, 1)
    )
    profile_slots = (
        jnp.zeros((4 * levels_here, tile_count * capacity), jnp.float32)
        .at[:, slot_ids]
        .set(kept_vals.reshape(4 * levels_here, cand_count))
    )
    partial_slots = (
        jnp.zeros((1, tile_count * capacity), jnp.float32).at[0, slot_ids].set(partial_value)
    )
    received, got_partial = (
        lax.all_to_all(profile_slots, "tile", split_axis=1, concat_axis=1, tiled=True),
        lax.all_to_all(partial_slots, "tile", split_axis=1, concat_axis=1, tiled=True),
    )
    sensitivity = lax.psum(got_partial, "depth")
    profiles = received.reshape(4, levels_here, 1, tile_count * capacity)
    return (fields, adjoint_now, profiles, sensitivity)


def solution(mesh):
    placed = (
        P(None, "depth", "tile", None),
        P(None, "depth", "tile", None),
        P("tile", None),
        P("tile", None),
        P("depth", "tile", None),
        P("depth", "tile", None),
        P("depth", "tile", None),
        P("tile"),
        P("tile", None),
        P("tile"),
        P("tile"),
    )
    return jax.shard_map(
        shards,
        mesh=mesh,
        in_specs=placed,
        out_specs=(
            P(None, "depth", "tile", None),
            P(None, "depth", "tile", None),
            P(None, "depth", "tile", None),
            P("tile", None),
        ),
        check_vma=False,
    )
```

profile of v0, /device:TPU:1, one launch (start us, length us, event | category | flops | bytes accessed | tf_op | source)
XLA Modules:
  0.0 297.0 jit_solution(681108002474564492)
XLA Ops:
  0.7 0.7 broadcast_compare_fusion
  1.4 0.8 fusion.98
  2.2 0.9 fusion.97
  3.1 1.0 fusion.91
  4.1 15.8 %all_gather.12 = f32[8,32,128]{2,1,0:T(8,128)S(1)} all-gather(f32[1,32,128]{2,1,0:T(8,128)S(1)} %slice.582), channel_id=1, replica_groups=mesh['tile'=32,'depth'=8] {'depth'}, dimensions={0}, use_global_device_ids=true | all-gather | bytes 147456 | tf_op jit(solution)/shard_map/all_gather | solution.py:33
  20.2 1.1 broadcast_multiply_fusion.1
  21.4 2.3 collective-permute-start.1
  23.7 1.3 collective-permute-start
  25.7 4.2 %collective-permute-start.9 = (f32[5,4,1,128]{3,2,1,0:T(1,128)}, f32[5,4,1,128]{3,2,1,0:T(1,128)S(1)}, u32[]{:S(2)}, u32[]{:S(2)}) collective-permute-start(f32[5,4,1,128]{3,2,1,0:T(1,128)} %get-tuple-element.513), channel_id=1, source_target_pairs={{0,8},{8,16},{16,24},{24,32},{32,40},{40,48},{48,56},{56,64},{64,7... | collective-permute-start | bytes 30728 | tf_op jit(solution)/shard_map/ppermute | solution.py:25
  29.8 1.3 collective-permute-start.8
  35.2 1.2 fusion.114
  36.4 1.1 fusion.113
  37.6 9.2 %reduce-window.6 = s32[32,32,128]{2,1,0:T(8,128)S(1)} reduce-window(s32[32,32,128]{2,1,0:T(8,128)S(1)} %fusion.6, s32[]{:T(128)} %constant.193.clone.1), window={size=1x1x128 pad=0_0x0_0x127_0}, to_apply=%region_12.13 | reduce-window | flops 16646144 | bytes 1048580 | tf_op jit(solution)/shard_map/reduce-window
  46.9 0.8 slice_reduce_fusion
  50.8 2.7 collective-permute-start.10
  53.5 2.8 collective-permute-start.11
  58.3 2.5 collective-permute-start.3
  60.8 2.6 collective-permute-start.2
  64.8 1.7 fusion.65
  66.4 1.5 reverse.8
  67.9 0.8 fusion.95
  68.8 13.3 %all_gather.14 = f32[8,32,128]{2,1,0:T(8,128)} all-gather(f32[1,32,128]{2,1,0:T(8,128)S(1)} %slice.630), channel_id=1, replica_groups=mesh['tile'=32,'depth'=8] {'depth'}, dimensions={0}, use_global_device_ids=true | all-gather | bytes 147456 | tf_op jit(solution)/shard_map/all_gather | solution.py:33
  82.1 5.8 %while.62 = (s32[]{:T(128)}, f32[32,128]{1,0:T(8,128)S(1)}, s32[]{:T(128)}, f32[8,32,128]{2,1,0:T(8,128)}, s32[]{:T(128)}, /*index=5*/s32[]{:T(128)}, s32[]{:T(128)}, s32[]{:T(128)}) while((s32[]{:T(128)}, f32[32,128]{1,0:T(8,128)S(1)}, s32[]{:T(128)}, f32[8,32,128]{2,1,0:T(8,128)}, s32[]{:T(128)}, /*index=5*/s32[]{:T(128)}, ...), condition=%wide.region_8.9_spmd.clone, body=%wide.region_7.8_spmd.clone.sunk | while | flops 12296 | bytes 49315 | solution.py:42
  82.1 0.7 add_select_fusion.10
  88.5 1.6 fusion.21
  90.2 0.9 fusion.68
  91.2 0.8 fusion.50
  91.9 1.6 fusion.41
  94.0 14.0 %all_gather.13 = f32[8,32,128]{2,1,0:T(8,128)} all-gather(f32[1,32,128]{2,1,0:T(8,128)S(1)} %slice.599), channel_id=1, replica_groups=mesh['tile'=32,'depth'=8] {'depth'}, dimensions={0}, use_global_device_ids=true | all-gather | bytes 147456 | tf_op jit(solution)/shard_map/all_gather | solution.py:33
  108.0 5.8 %while.61 = (s32[]{:T(128)}, f32[32,128]{1,0:T(8,128)S(1)}, s32[]{:T(128)}, f32[8,32,128]{2,1,0:T(8,128)}, s32[]{:T(128)}, /*index=5*/s32[]{:T(128)}) while((s32[]{:T(128)}, f32[32,128]{1,0:T(8,128)S(1)}, s32[]{:T(128)}, f32[8,32,128]{2,1,0:T(8,128)}, s32[]{:T(128)}, /*index=5*/s32[]{:T(128)}) %tuple.189), condition=%wide.region_5.6_spmd.clone, body=%wide.region_4.5_spmd.clone.sunk | while | flops 12292 | bytes 49253 | solution.py:42
  115.4 0.9 fusion.112
  116.3 0.9 fusion.111
  117.2 0.9 fusion.116
  118.0 0.9 fusion.115
  118.9 4.3 %collective-permute-start.13 = (f32[5,4,1,128]{3,2,1,0:T(1,128)S(1)}, f32[5,4,1,128]{3,2,1,0:T(1,128)S(1)}, u32[]{:S(2)}, u32[]{:S(2)}) collective-permute-start(f32[5,4,1,128]{3,2,1,0:T(1,128)S(1)} %get-tuple-element.511), channel_id=1, source_target_pairs={{0,8},{8,16},{16,24},{24,32},{32,40},{40,48},{48,56},{56,64},{64,7... | collective-permute-start | bytes 30728 | tf_op jit(solution)/shard_map/ppermute | solution.py:25
  123.2 1.3 collective-permute-start.12
  124.5 5.2 %collective-permute-start.5 = (f32[5,4,1,128]{3,2,1,0:T(1,128)S(1)}, f32[5,4,1,128]{3,2,1,0:T(1,128)S(1)}, u32[]{:S(2)}, u32[]{:S(2)}) collective-permute-start(f32[5,4,1,128]{3,2,1,0:T(1,128)S(1)} %get-tuple-element.515), channel_id=1, source_target_pairs={{0,8},{8,16},{16,24},{24,32},{32,40},{40,48},{48,56},{56,64},{64,7... | collective-permute-start | bytes 30728 | tf_op jit(solution)/shard_map/ppermute | solution.py:25
  129.7 1.3 collective-permute-start.4
  131.1 2.6 collective-permute-start.14
  133.7 3.2 %collective-permute-start.15 = (f32[5,1,34,128]{3,2,1,0:T(8,128)S(1)}, f32[5,1,34,128]{3,2,1,0:T(8,128)S(1)}, u32[]{:S(2)}, u32[]{:S(2)}) collective-permute-start(f32[5,1,34,128]{3,2,1,0:T(8,128)S(1)} %get-tuple-element.504), channel_id=1, source_target_pairs={{0,1},{1,2},{2,3},{3,4},{4,5},{5,6},{6,7},{8,9},{9,10},{10,11},{11... | collective-permute-start | bytes 261128 | tf_op jit(solution)/shard_map/ppermute | solution.py:25
  137.7 3.4 %collective-permute-start.7 = (f32[5,1,34,128]{3,2,1,0:T(8,128)}, f32[5,1,34,128]{3,2,1,0:T(8,128)}, u32[]{:S(2)}, u32[]{:S(2)}) collective-permute-start(f32[5,1,34,128]{3,2,1,0:T(8,128)} %get-tuple-element.507), channel_id=1, source_target_pairs={{0,1},{1,2},{2,3},{3,4},{4,5},{5,6},{6,7},{8,9},{9,10},{10,11},{11... | collective-permute-start | bytes 261128 | tf_op jit(solution)/shard_map/ppermute | solution.py:25
  141.1 1.9 collective-permute-start.6
  144.4 0.7 fusion.56
  145.1 1.5 reverse.9
  146.6 0.8 fusion.93
  148.0 14.0 %all_gather.15 = f32[8,32,128]{2,1,0:T(8,128)} all-gather(f32[1,32,128]{2,1,0:T(8,128)S(1)} %slice.649), channel_id=1, replica_groups=mesh['tile'=32,'depth'=8] {'depth'}, dimensions={0}, use_global_device_ids=true | all-gather | bytes 147456 | tf_op jit(solution)/shard_map/all_gather | solution.py:33
  162.0 5.8 %while.63 = (s32[]{:T(128)}, f32[32,128]{1,0:T(8,128)S(1)}, s32[]{:T(128)}, f32[8,32,128]{2,1,0:T(8,128)}, s32[]{:T(128)}, /*index=5*/s32[]{:T(128)}, s32[]{:T(128)}, s32[]{:T(128)}) while((s32[]{:T(128)}, f32[32,128]{1,0:T(8,128)S(1)}, s32[]{:T(128)}, f32[8,32,128]{2,1,0:T(8,128)}, s32[]{:T(128)}, /*index=5*/s32[]{:T(128)}, ...), condition=%wide.region_11.12_spmd.clone, body=%wide.region_10.11_spmd.clone.sunk | while | flops 12296 | bytes 49315 | solution.py:42
  162.0 0.7 add_select_fusion.11
  167.9 1.7 fusion.11
  169.6 0.9 fusion.59
  170.6 0.8 fusion.49
  171.4 1.2 fusion.31
  173.3 2.0 copy.42
  175.3 2.0 copy.46
  177.3 15.7 %gather_fusion = f32[4096,16]{1,0:T(8,128)} fusion(f32[16,4096]{0,1:T(8,128)} %copy.42, s32[4096]{0:T(1024)S(1)} %copy-done.26), kind=kCustom, calls=%fused_computation.clone | custom fusion | bytes 540672 | tf_op jit(solution)/shard_map/jit(_take)/gather | solution.py:171
  192.9 15.7 %gather_fusion.1 = f32[4096,16]{1,0:T(8,128)} fusion(f32[16,4096]{0,1:T(8,128)} %copy.46, s32[4096]{0:T(1024)S(1)} %copy-done.26), kind=kCustom, calls=%fused_computation.1.clone | custom fusion | bytes 540672 | tf_op jit(solution)/shard_map/jit(_take)/gather | solution.py:173
  208.6 2.8 fusion
  211.5 16.2 %scatter_custom_fusion.1 = f32[8192]{0:T(1024)} fusion(s32[4096]{0:T(1024)} %broadcast_select_fusion, f32[4096]{0:T(1024)S(1)} %broadcast_multiply_fusion.5, f32[]{:T(128)} %constant.192.clone.1), kind=kCustom, calls=%fused_computation.266 | custom fusion | bytes 33280
  227.7 14.7 %all-to-all-start.1 = ((f32[1,32,256]{2,0,1:T(1,128)}), f32[1,32,256]{2,0,1:T(1,128)S(1)}, u32[]{:S(2)}, u32[]{:S(2)}) async-start(f32[1,32,256]{2,0,1:T(1,128)} %bitcast.43), calls=%async_computation.1 | async-start | bytes 65536 | tf_op jit(solution)/shard_map/all_to_all | solution.py:189
  242.4 15.6 %scatter_custom_fusion = f32[16,8192]{0,1:T(8,128)} fusion(s32[4096]{0:T(1024)} %bitcast.183, f32[]{:T(128)} %constant.192.clone.1, f32[16,4096]{0,1:T(8,128)S(1)} %copy.43, f32[4096,16]{1,0:T(8,128)} %gather_fusion, f32[]{:T(128)} %constant.188.clone.2, pred[4096]{0:T(1024)(128)(4,1)S(1)} %copy-done.41), kind=kCustom, calls=%fused_computation.10 | custom fusion | flops 131072 | bytes 2888704 | tf_op jit(solution)/shard_map/scatter | solution.py:182
  258.0 3.5 %copy.44 = f32[16,32,256]{2,0,1:T(8,128)} copy(f32[16,32,256]{0,2,1:T(8,128)} %bitcast.175) | data formatting | bytes 1048576 | tf_op jit(solution)/shard_map/all_to_all | solution.py:188
  261.5 9.2 %all-to-all-start = ((f32[16,32,256]{2,0,1:T(8,128)}), f32[16,32,256]{2,0,1:T(8,128)S(1)}, u32[]{:S(2)}, u32[]{:S(2)}) async-start(f32[16,32,256]{2,0,1:T(8,128)} %copy.44), calls=%async_computation | async-start | bytes 1048576 | tf_op jit(solution)/shard_map/all_to_all | solution.py:188
  270.7 24.6 %psum.7 = f32[1,8192]{1,0:T(1,128)} all-reduce(f32[1,8192]{1,0:T(1,128)S(1)} %bitcast.184), channel_id=1, replica_groups=mesh['tile'=32,'depth'=8] {'depth'}, use_global_device_ids=true, to_apply=%region_18.20 | all-reduce | flops 8192 | bytes 65536 | tf_op jit(solution)/shard_map/psum | solution.py:191
  295.6 1.3 reshape.326
  (204 shorter events, 33.7 us)
Async XLA Ops:
  0.6 30.5 %copy-start.39 = (s32[4096]{0:T(1024)S(1)}, s32[4096]{0:T(1024)}, u32[]{:S(2)}) copy-start(s32[4096]{0:T(1024)} %param.28) | copy-start | bytes 49156
  21.4 35.0 %collective-permute-start.1 = (f32[5,4,1,128]{3,2,1,0:T(1,128)S(1)}, f32[5,4,1,128]{3,2,1,0:T(1,128)S(1)}, u32[]{:S(2)}, u32[]{:S(2)}) collective-permute-start(f32[5,4,1,128]{3,2,1,0:T(1,128)S(1)} %get-tuple-element.517), channel_id=1, source_target_pairs={{0,8},{8,16},{16,24},{24,32},{32,40},{40,48},{48,56},{56,64},{64,7... | collective-permute-start | bytes 30728 | tf_op jit(solution)/shard_map/ppermute | solution.py:25
  23.7 32.7 %collective-permute-start = (f32[5,4,1,128]{3,2,1,0:T(1,128)S(1)}, f32[5,4,1,128]{3,2,1,0:T(1,128)S(1)}, u32[]{:S(2)}, u32[]{:S(2)}) collective-permute-start(f32[5,4,1,128]{3,2,1,0:T(1,128)S(1)} %get-tuple-element.518), channel_id=1, source_target_pairs={{8,0},{16,8},{24,16},{32,24},{40,32},{48,40},{56,48},{64,56},{72,6... | collective-permute-start | bytes 30728 | tf_op jit(solution)/shard_map/ppermute | solution.py:26
  25.7 25.1 %collective-permute-start.9 = (f32[5,4,1,128]{3,2,1,0:T(1,128)}, f32[5,4,1,128]{3,2,1,0:T(1,128)S(1)}, u32[]{:S(2)}, u32[]{:S(2)}) collective-permute-start(f32[5,4,1,128]{3,2,1,0:T(1,128)} %get-tuple-element.513), channel_id=1, source_target_pairs={{0,8},{8,16},{16,24},{24,32},{32,40},{40,48},{48,56},{56,64},{64,7... | collective-permute-start | bytes 30728 | tf_op jit(solution)/shard_map/ppermute | solution.py:25
  29.8 20.9 %collective-permute-start.8 = (f32[5,4,1,128]{3,2,1,0:T(1,128)}, f32[5,4,1,128]{3,2,1,0:T(1,128)S(1)}, u32[]{:S(2)}, u32[]{:S(2)}) collective-permute-start(f32[5,4,1,128]{3,2,1,0:T(1,128)} %get-tuple-element.514), channel_id=1, source_target_pairs={{8,0},{16,8},{24,16},{32,24},{40,32},{48,40},{56,48},{64,56},{72,6... | collective-permute-start | bytes 30728 | tf_op jit(solution)/shard_map/ppermute | solution.py:26
  35.2 2.3 copy-start.40
  35.2 2.3 copy-start.42
  35.2 2.4 copy-start.27
  37.5 11.0 %copy-start.46 = (s32[2]{0:T(128)S(1)}, s32[2]{0:T(128)}, u32[]{:S(2)}) copy-start(s32[2]{0:T(128)} %constant.221) | copy-start | bytes 28
  37.5 11.1 %copy-start.45 = (s32[2]{0:T(128)S(1)}, s32[2]{0:T(128)}, u32[]{:S(2)}) copy-start(s32[2]{0:T(128)} %constant.218) | copy-start | bytes 28
  48.5 1.5 copy-start.28
  50.7 31.4 %copy-start.10 = (f32[32,128]{1,0:T(8,128)S(1)}, f32[32,128]{1,0:T(8,128)}, u32[]{:S(2)}) copy-start(f32[32,128]{1,0:T(8,128)} %custom-call.2) | copy-start | bytes 49156
  50.7 5.7 %copy-start.31 = (f32[5,4,1,128]{3,2,1,0:T(1,128)}, f32[5,4,1,128]{3,2,1,0:T(1,128)S(1)}, u32[]{:S(2)}) copy-start(f32[5,4,1,128]{3,2,1,0:T(1,128)S(1)} %collective-permute-done.9) | copy-start | bytes 30724
  50.8 5.7 %copy-start.32 = (f32[5,4,1,128]{3,2,1,0:T(1,128)}, f32[5,4,1,128]{3,2,1,0:T(1,128)S(1)}, u32[]{:S(2)}) copy-start(f32[5,4,1,128]{3,2,1,0:T(1,128)S(1)} %collective-permute-done.8) | copy-start | bytes 30724
  50.8 12.6 %collective-permute-start.10 = (f32[5,1,34,128]{3,2,1,0:T(8,128)S(1)}, f32[5,1,34,128]{3,2,1,0:T(8,128)S(1)}, u32[]{:S(2)}, u32[]{:S(2)}) collective-permute-start(f32[5,1,34,128]{3,2,1,0:T(8,128)S(1)} %get-tuple-element.505), channel_id=1, source_target_pairs={{1,0},{2,1},{3,2},{4,3},{5,4},{6,5},{7,6},{9,8},{10,9},{11,10},{12... | collective-permute-start | bytes 261128 | tf_op jit(solution)/shard_map/ppermute | solution.py:26
  53.5 9.9 %collective-permute-start.11 = (f32[5,1,34,128]{3,2,1,0:T(8,128)S(1)}, f32[5,1,34,128]{3,2,1,0:T(8,128)S(1)}, u32[]{:S(2)}, u32[]{:S(2)}) collective-permute-start(f32[5,1,34,128]{3,2,1,0:T(8,128)S(1)} %get-tuple-element.506), channel_id=1, source_target_pairs={{0,1},{1,2},{2,3},{3,4},{4,5},{5,6},{6,7},{8,9},{9,10},{10,11},{11... | collective-permute-start | bytes 261128 | tf_op jit(solution)/shard_map/ppermute | solution.py:25
  57.0 0.6 copy-start.30
  58.3 31.9 %copy-start.1 = (f32[4,32,128]{2,1,0:T(8,128)S(1)}, f32[4,32,128]{2,1,0:T(8,128)}, u32[]{:S(2)}) copy-start(f32[4,32,128]{2,1,0:T(8,128)} %param.26) | copy-start | bytes 196612
  58.3 31.9 %copy-start.2 = (f32[4,32,128]{2,1,0:T(8,128)S(1)}, f32[4,32,128]{2,1,0:T(8,128)}, u32[]{:S(2)}) copy-start(f32[4,32,128]{2,1,0:T(8,128)} %param.27) | copy-start | bytes 196612
  58.3 32.8 %collective-permute-start.3 = (f32[5,1,34,128]{3,2,1,0:T(8,128)}, f32[5,1,34,128]{3,2,1,0:T(8,128)}, u32[]{:S(2)}, u32[]{:S(2)}) collective-permute-start(f32[5,1,34,128]{3,2,1,0:T(8,128)} %get-tuple-element.509), channel_id=1, source_target_pairs={{0,1},{1,2},{2,3},{3,4},{4,5},{5,6},{6,7},{8,9},{9,10},{10,11},{11... | collective-permute-start | bytes 261128 | tf_op jit(solution)/shard_map/ppermute | solution.py:25
  60.8 30.3 %collective-permute-start.2 = (f32[5,1,34,128]{3,2,1,0:T(8,128)}, f32[5,1,34,128]{3,2,1,0:T(8,128)}, u32[]{:S(2)}, u32[]{:S(2)}) collective-permute-start(f32[5,1,34,128]{3,2,1,0:T(8,128)} %get-tuple-element.510), channel_id=1, source_target_pairs={{1,0},{2,1},{3,2},{4,3},{5,4},{6,5},{7,6},{9,8},{10,9},{11,10},{12... | collective-permute-start | bytes 261128 | tf_op jit(solution)/shard_map/ppermute | solution.py:26
  63.4 24.5 %copy-start.14 = (f32[5,1,34,128]{3,2,1,0:T(8,128)}, f32[5,1,34,128]{3,2,1,0:T(8,128)S(1)}, u32[]{:S(2)}) copy-start(f32[5,1,34,128]{3,2,1,0:T(8,128)S(1)} %collective-permute-done.10) | copy-start | bytes 261124
  63.4 0.7 copy-start.15
  68.7 19.1 %copy-start.17 = (f32[4,32,128]{2,1,0:T(8,128)}, f32[4,32,128]{2,1,0:T(8,128)S(1)}, u32[]{:S(2)}) copy-start(f32[4,32,128]{2,1,0:T(8,128)S(1)} %fusion.95) | copy-start | bytes 196612
  87.9 0.6 copy-start.11
  88.5 5.1 %copy-start = (f32[4,4,32,128]{3,2,1,0:T(8,128)S(1)}, f32[4,4,32,128]{3,2,1,0:T(8,128)}, u32[]{:S(2)}) copy-start(f32[4,4,32,128]{3,2,1,0:T(8,128)} %param.21) | copy-start | bytes 786436
  88.5 5.1 %copy-start.43 = (f32[32]{0:T(128)S(1)}, f32[32]{0:T(128)}, u32[]{:S(2)}) copy-start(f32[32]{0:T(128)} %sine_multiply_fusion) | copy-start | bytes 388
  90.1 3.5 %copy-start.18 = (f32[1,4,32,127]{3,2,1,0:T(8,128)S(1)}, f32[1,4,32,127]{3,2,1,0:T(8,128)}, u32[]{:S(2)}) copy-start(f32[1,4,32,127]{3,2,1,0:T(8,128)} %get-tuple-element.556) | copy-start | bytes 195076
  90.1 3.5 %copy-start.19 = (f32[1,4,32,127]{3,2,1,0:T(8,128)S(1)}, f32[1,4,32,127]{3,2,1,0:T(8,128)}, u32[]{:S(2)}) copy-start(f32[1,4,32,127]{3,2,1,0:T(8,128)} %get-tuple-element.557) | copy-start | bytes 195076
  90.2 3.5 %copy-start.20 = (f32[1,4,32,1]{3,2,1,0:T(8,128)S(1)}, f32[1,4,32,1]{3,2,1,0:T(8,128)}, u32[]{:S(2)}) copy-start(f32[1,4,32,1]{3,2,1,0:T(8,128)} %get-tuple-element.554) | copy-start | bytes 1540
  90.2 3.5 %copy-start.21 = (f32[1,4,32,1]{3,2,1,0:T(8,128)S(1)}, f32[1,4,32,1]{3,2,1,0:T(8,128)}, u32[]{:S(2)}) copy-start(f32[1,4,32,1]{3,2,1,0:T(8,128)} %get-tuple-element.555) | copy-start | bytes 1540
  118.0 44.0 %copy-start.9 = (f32[32,128]{1,0:T(8,128)S(1)}, f32[32,128]{1,0:T(8,128)}, u32[]{:S(2)}) copy-start(f32[32,128]{1,0:T(8,128)} %custom-call.3) | copy-start | bytes 49156
  118.9 12.1 %collective-permute-start.13 = (f32[5,4,1,128]{3,2,1,0:T(1,128)S(1)}, f32[5,4,1,128]{3,2,1,0:T(1,128)S(1)}, u32[]{:S(2)}, u32[]{:S(2)}) collective-permute-start(f32[5,4,1,128]{3,2,1,0:T(1,128)S(1)} %get-tuple-element.511), channel_id=1, source_target_pairs={{0,8},{8,16},{16,24},{24,32},{32,40},{40,48},{48,56},{56,64},{64,7... | collective-permute-start | bytes 30728 | tf_op jit(solution)/shard_map/ppermute | solution.py:25
  123.2 7.9 %collective-permute-start.12 = (f32[5,4,1,128]{3,2,1,0:T(1,128)S(1)}, f32[5,4,1,128]{3,2,1,0:T(1,128)S(1)}, u32[]{:S(2)}, u32[]{:S(2)}) collective-permute-start(f32[5,4,1,128]{3,2,1,0:T(1,128)S(1)} %get-tuple-element.512), channel_id=1, source_target_pairs={{8,0},{16,8},{24,16},{32,24},{40,32},{48,40},{56,48},{64,56},{72,6... | collective-permute-start | bytes 30728 | tf_op jit(solution)/shard_map/ppermute | solution.py:26
  124.5 12.4 %collective-permute-start.5 = (f32[5,4,1,128]{3,2,1,0:T(1,128)S(1)}, f32[5,4,1,128]{3,2,1,0:T(1,128)S(1)}, u32[]{:S(2)}, u32[]{:S(2)}) collective-permute-start(f32[5,4,1,128]{3,2,1,0:T(1,128)S(1)} %get-tuple-element.515), channel_id=1, source_target_pairs={{0,8},{8,16},{16,24},{24,32},{32,40},{40,48},{48,56},{56,64},{64,7... | collective-permute-start | bytes 30728 | tf_op jit(solution)/shard_map/ppermute | solution.py:25
  129.7 7.3 %collective-permute-start.4 = (f32[5,4,1,128]{3,2,1,0:T(1,128)S(1)}, f32[5,4,1,128]{3,2,1,0:T(1,128)S(1)}, u32[]{:S(2)}, u32[]{:S(2)}) collective-permute-start(f32[5,4,1,128]{3,2,1,0:T(1,128)S(1)} %get-tuple-element.516), channel_id=1, source_target_pairs={{8,0},{16,8},{24,16},{32,24},{40,32},{48,40},{56,48},{64,56},{72,6... | collective-permute-start | bytes 30728 | tf_op jit(solution)/shard_map/ppermute | solution.py:26
  131.0 13.3 %copy-start.37 = (f32[5,4,1,128]{3,2,1,0:T(1,128)}, f32[5,4,1,128]{3,2,1,0:T(1,128)S(1)}, u32[]{:S(2)}) copy-start(f32[5,4,1,128]{3,2,1,0:T(1,128)S(1)} %collective-permute-done.13) | copy-start | bytes 30724
  131.1 13.3 %copy-start.38 = (f32[5,4,1,128]{3,2,1,0:T(1,128)}, f32[5,4,1,128]{3,2,1,0:T(1,128)S(1)}, u32[]{:S(2)}) copy-start(f32[5,4,1,128]{3,2,1,0:T(1,128)S(1)} %collective-permute-done.12) | copy-start | bytes 30724
  131.1 12.0 %collective-permute-start.14 = (f32[5,1,34,128]{3,2,1,0:T(8,128)S(1)}, f32[5,1,34,128]{3,2,1,0:T(8,128)S(1)}, u32[]{:S(2)}, u32[]{:S(2)}) collective-permute-start(f32[5,1,34,128]{3,2,1,0:T(8,128)S(1)} %get-tuple-element.503), channel_id=1, source_target_pairs={{1,0},{2,1},{3,2},{4,3},{5,4},{6,5},{7,6},{9,8},{10,9},{11,10},{12... | collective-permute-start | bytes 261128 | tf_op jit(solution)/shard_map/ppermute | solution.py:26
  133.7 9.4 %collective-permute-start.15 = (f32[5,1,34,128]{3,2,1,0:T(8,128)S(1)}, f32[5,1,34,128]{3,2,1,0:T(8,128)S(1)}, u32[]{:S(2)}, u32[]{:S(2)}) collective-permute-start(f32[5,1,34,128]{3,2,1,0:T(8,128)S(1)} %get-tuple-element.504), channel_id=1, source_target_pairs={{0,1},{1,2},{2,3},{3,4},{4,5},{5,6},{6,7},{8,9},{9,10},{10,11},{11... | collective-permute-start | bytes 261128 | tf_op jit(solution)/shard_map/ppermute | solution.py:25
  137.0 6.1 %copy-start.33 = (f32[5,4,1,128]{3,2,1,0:T(1,128)}, f32[5,4,1,128]{3,2,1,0:T(1,128)S(1)}, u32[]{:S(2)}) copy-start(f32[5,4,1,128]{3,2,1,0:T(1,128)S(1)} %collective-permute-done.5) | copy-start | bytes 30724
  137.0 7.4 %copy-start.35 = (f32[5,4,1,128]{3,2,1,0:T(1,128)}, f32[5,4,1,128]{3,2,1,0:T(1,128)S(1)}, u32[]{:S(2)}) copy-start(f32[5,4,1,128]{3,2,1,0:T(1,128)S(1)} %collective-permute-done.4) | copy-start | bytes 30724
  137.7 32.8 %collective-permute-start.7 = (f32[5,1,34,128]{3,2,1,0:T(8,128)}, f32[5,1,34,128]{3,2,1,0:T(8,128)}, u32[]{:S(2)}, u32[]{:S(2)}) collective-permute-start(f32[5,1,34,128]{3,2,1,0:T(8,128)} %get-tuple-element.507), channel_id=1, source_target_pairs={{0,1},{1,2},{2,3},{3,4},{4,5},{5,6},{6,7},{8,9},{9,10},{10,11},{11... | collective-permute-start | bytes 261128 | tf_op jit(solution)/shard_map/ppermute | solution.py:25
  141.1 29.4 %collective-permute-start.6 = (f32[5,1,34,128]{3,2,1,0:T(8,128)}, f32[5,1,34,128]{3,2,1,0:T(8,128)}, u32[]{:S(2)}, u32[]{:S(2)}) collective-permute-start(f32[5,1,34,128]{3,2,1,0:T(8,128)} %get-tuple-element.508), channel_id=1, source_target_pairs={{1,0},{2,1},{3,2},{4,3},{5,4},{6,5},{7,6},{9,8},{10,9},{11,10},{12... | collective-permute-start | bytes 261128 | tf_op jit(solution)/shard_map/ppermute | solution.py:26
  143.1 0.6 copy-start.12
  143.7 0.6 copy-start.13
  147.4 0.6 copy-start.16
  167.8 2.7 copy-start.34
  167.8 2.7 copy-start.36
  167.8 3.5 %copy-start.5 = (f32[4,4,32,1]{3,2,1,0:T(8,128)S(1)}, f32[4,4,32,1]{3,2,1,0:T(8,128)}, u32[]{:S(2)}) copy-start(f32[4,4,32,1]{3,2,1,0:T(8,128)} %get-tuple-element.533) | copy-start | bytes 6148
  167.8 3.5 %copy-start.6 = (f32[4,4,32,1]{3,2,1,0:T(8,128)S(1)}, f32[4,4,32,1]{3,2,1,0:T(8,128)}, u32[]{:S(2)}) copy-start(f32[4,4,32,1]{3,2,1,0:T(8,128)} %get-tuple-element.534) | copy-start | bytes 6148
  167.8 3.5 %copy-start.7 = (f32[4,4,32,127]{3,2,1,0:T(8,128)S(1)}, f32[4,4,32,127]{3,2,1,0:T(8,128)}, u32[]{:S(2)}) copy-start(f32[4,4,32,127]{3,2,1,0:T(8,128)} %get-tuple-element.531) | copy-start | bytes 780292
  167.9 3.5 %copy-start.8 = (f32[4,4,32,127]{3,2,1,0:T(8,128)S(1)}, f32[4,4,32,127]{3,2,1,0:T(8,128)}, u32[]{:S(2)}) copy-start(f32[4,4,32,127]{3,2,1,0:T(8,128)} %get-tuple-element.532) | copy-start | bytes 780292
  167.9 4.7 %copy-start.44 = (f32[32]{0:T(128)S(1)}, f32[32]{0:T(128)}, u32[]{:S(2)}) copy-start(f32[32]{0:T(128)} %sine_multiply_fusion) | copy-start | bytes 388
  169.6 3.2 %copy-start.22 = (f32[1,4,32,127]{3,2,1,0:T(8,128)S(1)}, f32[1,4,32,127]{3,2,1,0:T(8,128)}, u32[]{:S(2)}) copy-start(f32[1,4,32,127]{3,2,1,0:T(8,128)} %get-tuple-element.552) | copy-start | bytes 195076
  169.6 3.1 %copy-start.23 = (f32[1,4,32,127]{3,2,1,0:T(8,128)S(1)}, f32[1,4,32,127]{3,2,1,0:T(8,128)}, u32[]{:S(2)}) copy-start(f32[1,4,32,127]{3,2,1,0:T(8,128)} %get-tuple-element.553) | copy-start | bytes 195076
  169.6 3.1 %copy-start.24 = (f32[1,4,32,1]{3,2,1,0:T(8,128)S(1)}, f32[1,4,32,1]{3,2,1,0:T(8,128)}, u32[]{:S(2)}) copy-start(f32[1,4,32,1]{3,2,1,0:T(8,128)} %get-tuple-element.550) | copy-start | bytes 1540
  169.6 3.1 %copy-start.25 = (f32[1,4,32,1]{3,2,1,0:T(8,128)S(1)}, f32[1,4,32,1]{3,2,1,0:T(8,128)}, u32[]{:S(2)}) copy-start(f32[1,4,32,1]{3,2,1,0:T(8,128)} %get-tuple-element.551) | copy-start | bytes 1540
  172.9 4.3 %copy-start.3 = (f32[4,4,32,128]{3,2,1,0:T(8,128)}, f32[4,4,32,128]{3,2,1,0:T(8,128)S(1)}, u32[]{:S(2)}) copy-start(f32[4,4,32,128]{3,2,1,0:T(8,128)S(1)} %pad_maximum_fusion.48) | copy-start | bytes 786436
  173.1 4.1 %copy-start.4 = (f32[4,4,32,128]{3,2,1,0:T(8,128)}, f32[4,4,32,128]{3,2,1,0:T(8,128)S(1)}, u32[]{:S(2)}) copy-start(f32[4,4,32,128]{3,2,1,0:T(8,128)S(1)} %maximum_multiply_fusion.1) | copy-start | bytes 786436
  173.3 4.0 %copy-start.26 = (s32[4096]{0:T(1024)S(1)}, s32[4096]{0:T(1024)}, u32[]{:S(2)}) copy-start(s32[4096]{0:T(1024)} %fusion.108) | copy-start | bytes 49156
  177.3 31.4 %copy-start.41 = (pred[4096]{0:T(1024)(128)(4,1)S(1)}, pred[4096]{0:T(1024)(128)(4,1)}, u32[]{:S(2)}) copy-start(pred[4096]{0:T(1024)(128)(4,1)} %compare_and_fusion.1) | copy-start | bytes 12292
  227.7 33.8 %all-to-all-start.1 = ((f32[1,32,256]{2,0,1:T(1,128)}), f32[1,32,256]{2,0,1:T(1,128)S(1)}, u32[]{:S(2)}, u32[]{:S(2)}) async-start(f32[1,32,256]{2,0,1:T(1,128)} %bitcast.43), calls=%async_computation.1 | async-start | bytes 65536 | tf_op jit(solution)/shard_map/all_to_all | solution.py:189
  261.5 33.9 %all-to-all-start = ((f32[16,32,256]{2,0,1:T(8,128)}), f32[16,32,256]{2,0,1:T(8,128)S(1)}, u32[]{:S(2)}, u32[]{:S(2)}) async-start(f32[16,32,256]{2,0,1:T(8,128)} %copy.44), calls=%async_computation | async-start | bytes 1048576 | tf_op jit(solution)/shard_map/all_to_all | solution.py:188
  (1 other events, 0.6 us)
where the time goes:
time: 302 us; the launch traced here: 297 us
  blocking collectives  81.7 us (27%)
  local copies, waits for them, and re-layouts  76.1 us (25%)
  other arithmetic  70.4 us (23%)
  starting transfers between devices  66.8 us (22%)
    all_gather x4, blocking collectives, prefix(): everything = lax.all_gather(x, axis)  57.1 us
    ppermute x8, starting transfers between devices, padded_2(): before = lax.ppermute(last, axis, up)  27.9 us
    psum x1, blocking collectives, shards(): sensitivity = lax.psum(got_partial, 'depth')  24.6 us
    unnamed x97, local copies, waits for them, and re-layouts  21 us
    select_n x32, other arithmetic, lap(): return jnp.where(reached, new, before)  17.4 us
    gather x1, local copies, waits for them, and re-layouts, shards(): jnp.take(fields.reshape(4 * levels_here, rows_here * width), columns, axi...  15.7 us
    gather x1, local copies, waits for them, and re-layouts, shards(): jnp.take(adjoint_now.reshape(4 * levels_here, rows_here * width), columns...  15.7 us
    scatter x1, other arithmetic, shards(): profile_slots = jnp.zeros((4 * levels_here, tile_count * capacity), jnp.f...  15.6 us
  transfers between devices with their start and end apart: 18, of which 0 were waited for; matrix products, arithmetic and copies ran while one was open for 22% of the time, Pallas kernels for 0%

commit v1 on v0

v1 whole, which is shorter than its diff:
```python
import functools
import math

import jax
import jax.numpy as jnp
from jax import lax
from jax.experimental import pallas as pl
from jax.experimental.pallas import tpu as pltpu
from jax.sharding import PartitionSpec as P

STEPS = 2
LANES = 128

nu_horiz = 0.06
nu_vert = 0.08
press_coef = 0.1
grav_step = 0.2
sens_scale = 0.2

MESH = pl.DeviceIdType.MESH
F32 = jnp.float32
BF16 = jnp.bfloat16
I32 = jnp.int32


def iota(shape, dim):
    return lax.broadcasted_iota(I32, shape, dim)


def lane_diff(p):
    return 0.5 * (pltpu.roll(p, p.shape[1] - 1, 1) - pltpu.roll(p, 1, 1))


def row_after(p, bottom):
    rows = p.shape[0]
    return jnp.where(iota(p.shape, 0) == rows - 1, bottom, pltpu.roll(p, rows - 1, 0))


def row_before(p, top):
    return jnp.where(iota(p.shape, 0) == 0, top, pltpu.roll(p, 1, 0))


def kernel(
    tiles,
    depths,
    pert,
    cot,
    land,
    bottom,
    gain,
    expan,
    contr,
    cols,
    owns,
    starts,
    counts,
    fin_out,
    adj_out,
    prof_out,
    sens_out,
    wet,
    gw,
    fin,
    mid,
    amid,
    act,
    qf,
    qb,
    runs,
    edge_out,
    edge_in,
    tot_out,
    tot_in,
    diag_out,
    diag_in,
    rank_in,
    ranks,
    hot_own,
    hot_rank,
    lane_tab,
    row_tab,
    lev_tab,
    cells,
    sens_cells,
    send_buf,
    sens_part,
    sens_peer,
    sens_send,
    q_send,
    q_recv,
    e_send,
    e_recv,
    t_send,
    t_recv,
    d_send,
    d_recv,
    p_sem,
    s_sem,
    x_send,
    x_recv,
):
    levels, rows = wet.shape[0], wet.shape[1]
    cap = ranks_cap = hot_rank.shape[0]
    halves = cap // LANES
    chunks = owns.shape[0]
    planes = 4 * levels
    t = lax.axis_index("tile")
    d = lax.axis_index("depth")

    barrier = pltpu.get_barrier_semaphore()

    def greet(to_tile, to_depth):
        pl.semaphore_signal(barrier, inc=1, device_id=(to_tile, to_depth), device_id_type=MESH)

    def greet_depths(j, _):
        peer = lax.rem(d + j, depths)
        greet(t, peer)

        @pl.when(t > 0)
        def _():
            greet(t - 1, peer)

        @pl.when(t < tiles - 1)
        def _():
            greet(t + 1, peer)

        return 0

    lax.fori_loop(1, depths, greet_depths, 0)

    def greet_tiles(j, _):
        greet(lax.rem(t + j, tiles), d)
        return 0

    lax.fori_loop(1, tiles, greet_tiles, 0)

    zero_plane = jnp.zeros((rows, LANES), F32)
    ocean = land[...] == 1
    for k in range(levels):
        w = jnp.where(ocean & (d * levels + k < bottom[...]), 1.0, 0.0).astype(F32)
        wet[k] = w
        gw[k] = w * gain[k]

    @pl.when(d == 0)
    def _():
        for s in range(2):
            for f in range(4):
                qf[s, f, 0] = zero_plane
                qb[s, f, 0] = zero_plane

    @pl.when(d == depths - 1)
    def _():
        for s in range(2):
            for f in range(4):
                qf[s, f, levels + 1] = zero_plane
                qb[s, f, levels + 1] = zero_plane

    def clear_side(side):
        for rnd in range(4):
            edge_in[rnd, side] = jnp.zeros(edge_in.shape[2:], F32)
            diag_in[rnd, side] = jnp.zeros(diag_in.shape[2:], F32)

    @pl.when(t == 0)
    def _():
        clear_side(0)

    @pl.when(t == tiles - 1)
    def _():
        clear_side(1)

    def store_edges(rnd, at, plane):
        edge_out[rnd, 0, at : at + 1] = plane[0:1]
        edge_out[rnd, 1, at : at + 1] = plane[rows - 1 : rows]

    def prepare_forward(src, s, rnd):
        running = zero_plane
        for k in range(levels):
            running = running + (contr[k] * src[1, k] - expan[k] * src[0, k])
            runs[rnd, k] = running
            store_edges(rnd, planes + k, running)
        tot_out[rnd] = running
        diag_out[rnd, 0] = running[0:1]
        diag_out[rnd, 1] = running[rows - 1 : rows]
        for f in range(4):
            for k in range(levels):
                q = gw[k] * src[f, k]
                qf[s, f, k + 1] = q
                store_edges(rnd, f * levels + k, q)

    def prepare_backward(src, s, rnd):
        run_u = zero_plane
        run_v = zero_plane
        zero_row = jnp.zeros((1, LANES), F32)
        for k in reversed(range(levels)):
            run_u = run_u + wet[k] * src[2, k]
            run_v = run_v + wet[k] * src[3, k]
            store_edges(rnd, planes + k, run_v)
            runs[rnd, k] = lane_diff(run_u) + 0.5 * (
                row_after(run_v, zero_row) - row_before(run_v, zero_row)
            )
        tot_out[rnd] = runs[rnd, 0]
        diag_out[rnd, 0] = run_v[0:1]
        diag_out[rnd, 1] = run_v[rows - 1 : rows]
        for f in range(4):
            for k in range(levels):
                a = wet[k] * src[f, k]
                act[s, f, k] = a
                q = gw[k] * a
                qb[s, f, k + 1] = q
                store_edges(rnd, f * levels + k, q)

    def remote(src, dst, send, recv, to_tile, to_depth):
        return pltpu.make_async_remote_copy(
            src_ref=src,
            dst_ref=dst,
            send_sem=send,
            recv_sem=recv,
            device_id=(to_tile, to_depth),
            device_id_type=MESH,
        )

    def level_up(q, s, rnd):
        return remote(
            q.at[s, :, levels], q.at[s, :, 0], q_send.at[rnd, 1], q_recv.at[rnd, 0], t, d + 1
        )

    def level_down(q, s, rnd):
        return remote(
            q.at[s, :, 1], q.at[s, :, levels + 1], q_send.at[rnd, 0], q_recv.at[rnd, 1], t, d - 1
        )

    def edge_copy(rnd, side):
        return remote(
            edge_out.at[rnd, side],
            edge_in.at[rnd, 1 - side],
            e_send.at[rnd, side],
            e_recv.at[rnd, 1 - side],
            t - 1 if side == 0 else t + 1,
            d,
        )

    def tot_copy(rnd, peer, slot):
        return remote(
            tot_out.at[rnd], tot_in.at[rnd, slot], t_send.at[rnd, peer], t_recv.at[rnd, slot], t, peer
        )

    def diag_copy(rnd, side, peer, slot):
        return remote(
            diag_out.at[rnd, side],
            diag_in.at[rnd, 1 - side, slot],
            d_send.at[rnd, side, peer],
            d_recv.at[rnd, 1 - side, slot],
            t - 1 if side == 0 else t + 1,
            peer,
        )

    has_side = (t > 0, t < tiles - 1)

    def ahead(forward):
        return (d + 1, depths) if forward else (0, d)

    def behind(forward):
        return (0, d) if forward else (d + 1, depths)

    def send_round(q, s, rnd, forward):
        @pl.when(d < depths - 1)
        def _():
            level_up(q, s, rnd).start()

        @pl.when(d > 0)
        def _():
            level_down(q, s, rnd).start()

        def one(peer, _):
            tot_copy(rnd, peer, d).start()
            for side in range(2):

                @pl.when(has_side[side])
                def _():
                    diag_copy(rnd, side, peer, d).start()

            return 0

        for side in range(2):

            @pl.when(has_side[side])
            def _():
                edge_copy(rnd, side).start()

        lax.fori_loop(*ahead(forward), one, 0)

    def recv_round(q, s, rnd, forward):
        def one(peer, _):
            tot_copy(rnd, peer, peer).wait_recv()
            for side in range(2):

                @pl.when(has_side[1 - side])
                def _():
                    diag_copy(rnd, side, peer, peer).wait_recv()

            return 0

        lax.fori_loop(*behind(forward), one, 0)
        for side in range(2):

            @pl.when(has_side[1 - side])
            def _():
                edge_copy(rnd, side).wait_recv()

        @pl.when(d > 0)
        def _():
            level_up(q, s, rnd).wait_recv()

        @pl.when(d < depths - 1)
        def _():
            level_down(q, s, rnd).wait_recv()

    def drain_round(q, s, rnd, forward):
        def one(peer, _):
            tot_copy(rnd, peer, d).wait_send()
            for side in range(2):

                @pl.when(has_side[side])
                def _():
                    diag_copy(rnd, side, peer, d).wait_send()

            return 0

        lax.fori_loop(*ahead(forward), one, 0)
        for side in range(2):

            @pl.when(has_side[side])
            def _():
                edge_copy(rnd, side).wait_send()

        @pl.when(d < depths - 1)
        def _():
            level_up(q, s, rnd).wait_send()

        @pl.when(d > 0)
        def _():
            level_down(q, s, rnd).wait_send()

    def base_sums(rnd, forward):
        def one(peer, carry):
            base, top, low = carry
            return (
                base + tot_in[rnd, peer],
                top + diag_in[rnd, 0, peer],
                low + diag_in[rnd, 1, peer],
            )

        zero_row = jnp.zeros((1, LANES), F32)
        return lax.fori_loop(*behind(forward), one, (zero_plane, zero_row, zero_row))

    def mixed(q, s, rnd, f, k):
        c = q[s, f, k + 1]
        at = f * levels + k
        north = row_after(c, edge_in[rnd, 1, at : at + 1])
        south = row_before(c, edge_in[rnd, 0, at : at + 1])
        horizontal = (
            north + south + pltpu.roll(c, 1, 1) + pltpu.roll(c, LANES - 1, 1) - 4.0 * c
        )
        vertical = q[s, f, k + 2] + q[s, f, k] - 2.0 * c
        return gw[k] * (nu_horiz * horizontal + nu_vert * vertical)

    row_ids = (t * rows + iota((rows, LANES), 0)).astype(F32)
    coriolis = 0.4 * jnp.sin(math.pi * ((row_ids + 0.5) / (tiles * rows) - 0.5))

    def finish_forward(src, s, rnd, store):
        base, top, low = base_sums(rnd, True)
        for k in range(levels):
            at = planes + k
            p = grav_step * (base + runs[rnd, k])
            p_top = grav_step * (top + edge_in[rnd, 0, at : at + 1])
            p_low = grav_step * (low + edge_in[rnd, 1, at : at + 1])
            gy = 0.5 * (row_after(p, p_low) - row_before(p, p_top))
            w = wet[k]
            for f in range(2):
                store(f, k, w * (src[f, k] + mixed(qf, s, rnd, f, k)))
            u, v = src[2, k], src[3, k]
            store(2, k, w * (u + mixed(qf, s, rnd, 2, k) + coriolis * v - press_coef * lane_diff(p)))
            store(3, k, w * (v + mixed(qf, s, rnd, 3, k) - coriolis * u - press_coef * gy))

    def finish_backward(s, rnd, store):
        base, top, low = base_sums(rnd, False)
        for k in range(levels):
            at = planes + k
            v_top = top + edge_in[rnd, 0, at : at + 1]
            v_low = low + edge_in[rnd, 1, at : at + 1]
            row = iota((rows, LANES), 0)
            rim = jnp.where(row == 0, -0.5 * v_top, 0.0) + jnp.where(row == rows - 1, 0.5 * v_low, 0.0)
            dens = (grav_step * press_coef) * (base + runs[rnd, k] + rim)
            a_t, a_s, a_u, a_v = (act[s, f, k] for f in range(4))
            store(0, k, a_t + mixed(qb, s, rnd, 0, k) - expan[k] * dens)
            store(1, k, a_s + mixed(qb, s, rnd, 1, k) + contr[k] * dens)
            store(2, k, a_u + mixed(qb, s, rnd, 2, k) - coriolis * a_v)
            store(3, k, a_v + mixed(qb, s, rnd, 3, k) + coriolis * a_u)

    prepare_forward(pert, 0, 0)
    prepare_backward(cot, 0, 1)

    sides = has_side[0].astype(I32) + has_side[1].astype(I32)
    pl.semaphore_wait(barrier, (depths - 1) * (1 + sides) + tiles - 1)

    send_round(qf, 0, 0, True)
    send_round(qb, 0, 1, False)

    own_ids = iota((tiles, LANES), 0)

    def rank_inputs(i, before):
        hot = (owns[pl.ds(i, 1), :] == own_ids).astype(F32)
        at = pl.multiple_of(i * tiles, tiles)
        rank_in[pl.ds(at, tiles), 0:LANES] = hot.astype(BF16)
        rank_in[pl.ds(at, tiles), LANES : 2 * LANES] = before.astype(BF16)
        return before + hot

    lax.fori_loop(0, chunks, rank_inputs, jnp.zeros((tiles, LANES), F32))
    i_row, i_col = iota((2 * LANES, LANES), 0), iota((2 * LANES, LANES), 1)
    earlier = jnp.where((i_row < i_col) | (i_row >= LANES), 1.0, 0.0).astype(BF16)
    ranks[...] = jnp.dot(rank_in[...], earlier, preferred_element_type=F32)
    slot_ids = iota((cap, LANES), 0)

    def slot_inputs(i, _):
        hot = (owns[pl.ds(i, 1), :] == own_ids).astype(F32)
        at = pl.multiple_of(i * tiles, tiles)
        lanes = pl.ds(pl.multiple_of(i * LANES, LANES), LANES)
        rank = jnp.sum(hot * ranks[pl.ds(at, tiles), :], axis=0, keepdims=True).astype(I32)
        hot_rank[:, lanes] = (slot_ids == rank).astype(F32).astype(BF16)
        c = cols[pl.ds(i, 1), :]
        lane = (c & (LANES - 1)).astype(F32)
        row = ((c >> 7) + 32).astype(F32)
        lev = (starts[pl.ds(i, 1), :] * 16 + counts[pl.ds(i, 1), :] - 1).astype(F32)
        hot_own[0:tiles, lanes] = (hot * lane).astype(BF16)
        hot_own[tiles : 2 * tiles, lanes] = (hot * row).astype(BF16)
        hot_own[2 * tiles : 3 * tiles, lanes] = (hot * lev).astype(BF16)
        return 0

    lax.fori_loop(0, chunks, slot_inputs, 0)
    table = lax.dot_general(
        hot_own[...], hot_rank[...], (((1,), (1,)), ((), ())), preferred_element_type=F32
    ).astype(I32)
    for h in range(halves):
        part = table[:, h * LANES : (h + 1) * LANES]
        lane_tab[h * tiles : (h + 1) * tiles] = part[0:tiles]
        row_tab[h * tiles : (h + 1) * tiles] = part[tiles : 2 * tiles] - 32
        lev_tab[h * tiles : (h + 1) * tiles] = part[2 * tiles : 3 * tiles]

    def store_mid(f, k, value):
        mid[f, k] = value

    def store_fin(f, k, value):
        fin_out[f, k] = value
        fin[(f * levels + k) * rows : (f * levels + k + 1) * rows] = value

    def store_amid(f, k, value):
        amid[f, k] = value

    def store_adj(f, k, value):
        adj_out[f, k] = value

    recv_round(qf, 0, 0, True)
    finish_forward(pert, 0, 0, store_mid)
    prepare_forward(mid, 1, 2)
    send_round(qf, 1, 2, True)
    recv_round(qb, 0, 1, False)
    finish_backward(0, 1, store_amid)
    prepare_backward(amid, 1, 3)
    send_round(qb, 1, 3, False)
    recv_round(qf, 1, 2, True)
    finish_forward(mid, 1, 2, store_fin)

    groups = planes // 8
    for g in range(groups):
        for r in range(rows):
            cells[r, g * 8 : g * 8 + 8] = fin[pl.ds(g * 8 * rows + r, 8, stride=rows), :]

    sub = iota((8, LANES), 0)
    level_ids = d * levels + lax.rem(sub, levels)

    def profile_copy(owner):
        return remote(
            send_buf.at[owner],
            prof_out.at[:, pl.ds(pl.multiple_of(t * cap, LANES), cap)],
            p_sem.at[0],
            p_sem.at[1],
            owner,
            d,
        )

    def gather_owner(j, _):
        owner = lax.rem(t + j, tiles)
        for h in range(halves):
            at = pl.ds(h * tiles + owner, 1)
            lane = jnp.broadcast_to(lane_tab[at, :], (8, LANES))
            row = jnp.broadcast_to(row_tab[at, :], (8, LANES))
            lev = jnp.broadcast_to(lev_tab[at, :], (8, LANES))
            first = lev >> 4
            kept = (level_ids >= first) & (level_ids <= first + (lev & 15))
            row = jnp.where(kept, row, -1)
            totals = [jnp.zeros((8, LANES), F32)] * groups
            for r in range(rows):
                here = row == r
                for g in range(groups):
                    got = jnp.take_along_axis(
                        cells[r, g * 8 : g * 8 + 8], lane, axis=1, mode="promise_in_bounds"
                    )
                    totals[g] = jnp.where(here, got, totals[g])
            for g in range(groups):
                send_buf[owner, g * 8 : g * 8 + 8, h * LANES : (h + 1) * LANES] = totals[g]

        @pl.when(j > 0)
        def _():
            profile_copy(owner).start()

        return 0

    lax.fori_loop(0, tiles, gather_owner, 0)
    own_copy = pltpu.make_async_copy(
        send_buf.at[t],
        prof_out.at[:, pl.ds(pl.multiple_of(t * cap, LANES), cap)],
        x_send.at[0],
    )
    own_copy.start()

    recv_round(qb, 1, 3, False)
    finish_backward(1, 3, store_adj)

    for k in range(levels):
        total = zero_plane
        for f in range(4):
            total = total + fin_out[f, k] * adj_out[f, k]
        runs[0, k] = total
    pairs = 8 // levels
    for r in range(rows // pairs):
        for k in range(levels):
            for h in range(pairs):
                at = r + h * (rows // pairs)
                sens_cells[r, k * pairs + h : k * pairs + h + 1] = runs[0, k, at : at + 1]

    sub_level = d * levels + sub // pairs
    sub_row = lax.rem(sub, pairs) * (rows // pairs)

    def gather_sens(owner, _):
        for h in range(halves):
            at = pl.ds(h * tiles + owner, 1)
            lane = jnp.broadcast_to(lane_tab[at, :], (8, LANES))
            row = jnp.broadcast_to(row_tab[at, :], (8, LANES)) - sub_row
            lev = jnp.broadcast_to(lev_tab[at, :], (8, LANES))
            first = lev >> 4
            kept = (sub_level >= first) & (sub_level <= first + (lev & 15))
            row = jnp.where(kept, row, -1)
            total = jnp.zeros((8, LANES), F32)
            for r in range(rows // pairs):
                got = jnp.take_along_axis(sens_cells[r], lane, axis=1, mode="promise_in_bounds")
                total = jnp.where(row == r, got, total)
            sens_part[at, :] = sens_scale * jnp.sum(total, axis=0, keepdims=True)
        return 0

    lax.fori_loop(0, tiles, gather_sens, 0)

    def sens_exchange(peer, slot):
        return remote(sens_part, sens_peer.at[slot], x_send.at[1 + peer], x_recv.at[slot], t, peer)

    def start_exchange(j, _):
        sens_exchange(lax.rem(d + j, depths), d).start()
        return 0

    def wait_exchange(j, total):
        peer = lax.rem(d + j, depths)
        sens_exchange(peer, peer).wait_recv()
        return total + sens_peer[peer]

    lax.fori_loop(1, depths, start_exchange, 0)
    total = lax.fori_loop(1, depths, wait_exchange, sens_part[...])
    for o in range(tiles):
        for h in range(halves):
            sens_send[o, :, h * LANES : (h + 1) * LANES] = total[h * tiles + o : h * tiles + o + 1]

    mine = pl.ds(pl.multiple_of(t * cap, LANES), cap)

    def sens_copy(owner):
        return remote(
            sens_send.at[owner], sens_out.at[:, mine], s_sem.at[0], s_sem.at[1], owner, d
        )

    def start_sens(j, _):
        sens_copy(lax.rem(t + j, tiles)).start()
        return 0

    lax.fori_loop(1, tiles, start_sens, 0)
    own_sens = pltpu.make_async_copy(sens_send.at[t], sens_out.at[:, mine], x_recv.at[d])
    own_sens.start()

    drain_round(qf, 0, 0, True)
    drain_round(qb, 0, 1, False)
    drain_round(qf, 1, 2, True)
    drain_round(qb, 1, 3, False)

    def drain_exchange(j, _):
        sens_exchange(lax.rem(d + j, depths), d).wait_send()
        return 0

    lax.fori_loop(1, depths, drain_exchange, 0)
    own_copy.wait()
    own_sens.wait()
    for buf, sems in ((send_buf, p_sem), (sens_send, s_sem)):
        all_but_one = buf.at[pl.ds(0, tiles - 1)]
        for way in range(2):
            pltpu.make_async_copy(all_but_one, all_but_one, sems.at[way]).wait()


def shards(
    perturbation,
    cotangent,
    land_mask,
    bottom_level,
    mix_gain,
    expansion,
    contraction,
    columns,
    owners,
    level_start,
    level_count,
):
    tiles, depths = lax.axis_size("tile"), lax.axis_size("depth")
    levels, rows, width = perturbation.shape[1:]
    cand = columns.shape[0]
    chunks = cand // LANES
    cap = 2 * cand // tiles
    planes = 4 * levels
    edge_rows = -(-(planes + levels) // 8) * 8

    def listed(x):
        return x.reshape(chunks, LANES)

    vmem = pl.BlockSpec(memory_space=pltpu.VMEM)
    hbm = pl.BlockSpec(memory_space=pl.ANY)
    state = (4, levels, rows, width)
    dma = pltpu.SemaphoreType.DMA
    final, adjoint, profiles, sensitivity = pl.pallas_call(
        functools.partial(kernel, tiles, depths),
        out_shape=(
            jax.ShapeDtypeStruct(state, F32),
            jax.ShapeDtypeStruct(state, F32),
            jax.ShapeDtypeStruct((planes, tiles * cap), F32),
            jax.ShapeDtypeStruct((1, tiles * cap), F32),
        ),
        in_specs=[vmem] * 11,
        out_specs=(vmem, vmem, hbm, hbm),
        scratch_shapes=[
            pltpu.VMEM((levels, rows, width), F32),
            pltpu.VMEM((levels, rows, width), F32),
            pltpu.VMEM((planes * rows, width), F32),
            pltpu.VMEM(state, F32),
            pltpu.VMEM(state, F32),
            pltpu.VMEM((2,) + state, F32),
            pltpu.VMEM((2, 4, levels + 2, rows, width), F32),
            pltpu.VMEM((2, 4, levels + 2, rows, width), F32),
            pltpu.VMEM((4, levels, rows, width), F32),
            pltpu.VMEM((4, 2, edge_rows, width), F32),
            pltpu.VMEM((4, 2, edge_rows, width), F32),
            pltpu.VMEM((4, rows, width), F32),
            pltpu.VMEM((4, depths, rows, width), F32),
            pltpu.VMEM((4, 2, 1, width), F32),
            pltpu.VMEM((4, 2, depths, 1, width), F32),
            pltpu.VMEM((chunks * tiles, 2 * LANES), BF16),
            pltpu.VMEM((chunks * tiles, LANES), F32),
            pltpu.VMEM((3 * tiles, cand), BF16),
            pltpu.VMEM((cap, cand), BF16),
            pltpu.VMEM((cap // LANES * tiles, LANES), I32),
            pltpu.VMEM((cap // LANES * tiles, LANES), I32),
            pltpu.VMEM((cap // LANES * tiles, LANES), I32),
            pltpu.VMEM((rows, planes, width), F32),
            pltpu.VMEM((rows * levels // 8, 8, width), F32),
            pltpu.VMEM((tiles, planes, cap), F32),
            pltpu.VMEM((cap // LANES * tiles, LANES), F32),
            pltpu.VMEM((depths, cap // LANES * tiles, LANES), F32),
            pltpu.VMEM((tiles, 1, cap), F32),
            dma((4, 2)),
            dma((4, 2)),
            dma((4, 2)),
            dma((4, 2)),
            dma((4, depths)),
            dma((4, depths)),
            dma((4, 2, depths)),
            dma((4, 2, depths)),
            dma((2,)),
            dma((2,)),
            dma((1 + depths,)),
            dma((depths,)),
        ],
        compiler_params=pltpu.CompilerParams(
            collective_id=0, has_side_effects=True, vmem_limit_bytes=32 * 1024 * 1024
        ),
    )(
        perturbation,
        cotangent,
        land_mask,
        bottom_level,
        mix_gain,
        expansion,
        contraction,
        listed(columns),
        listed(owners),
        listed(level_start),
        listed(level_count),
    )
    return final, adjoint, profiles.reshape(4, levels, 1, tiles * cap), sensitivity


def solution(mesh):
    placed = (
        P(None, "depth", "tile", None),
        P(None, "depth", "tile", None),
        P("tile", None),
        P("tile", None),
        P("depth", "tile", None),
        P("depth", "tile", None),
        P("depth", "tile", None),
        P("tile"),
        P("tile", None),
        P("tile"),
        P("tile"),
    )
    return jax.shard_map(
        shards,
        mesh=mesh,
        in_specs=placed,
        out_specs=(
            P(None, "depth", "tile", None),
            P(None, "depth", "tile", None),
            P(None, "depth", "tile", None),
            P("tile", None),
        ),
        check_vma=False,
    )
```

time: 302 us -> 57.1 us (0.19); the launches traced: 297 us -> 56.5 us
  blocking collectives: 81.7 us -> 0 us
  other arithmetic: 70.4 us -> 0 us
  starting transfers between devices: 66.8 us -> 0 us
  local copies, waits for them, and re-layouts: 76.1 us -> 12.1 us
  Pallas kernels: 0 us -> 43.7 us
    all_gather x4 -> x0, blocking collectives: 57.1 us -> none  [prefix(): everything = lax.all_gather(x, axis)]
    pallas_call x0 -> x1, Pallas kernels: none -> 43.7 us  [shards(): pl.pallas_call(functools.partial(kernel, tiles, depths), out_shape=(jax.S...]
    ppermute x16 -> x0, starting transfers between devices: 42.9 us -> none  [the longest x8 27.9 us: padded_2(): before = lax.ppermute(last, axis, up)]
    gather x2 -> x0, local copies, waits for them, and re-layouts: 31.4 us -> none  [the longest x1 15.7 us: shards(): jnp.take(fields.reshape(4 * levels_here, rows_here * width), columns, axi...]
    psum x1 -> x0, blocking collectives: 24.6 us -> none  [shards(): sensitivity = lax.psum(got_partial, 'depth')]
    all_to_all x2 -> x0, starting transfers between devices: 23.9 us -> none  [the longest x1 14.7 us: shards(): lax.all_to_all(partial_slots, 'tile', split_axis=1, concat_axis=1, tiled=...]
    select_n x33 -> x0, other arithmetic: 17.4 us -> none  [the longest x32 17.4 us: lap(): return jnp.where(reached, new, before)]
    scatter x1 -> x0, other arithmetic: 15.6 us -> none  [shards(): profile_slots = jnp.zeros((4 * levels_here, tile_count * capacity), jnp.f...]
  transfers between devices with their start and end apart: 18 -> 0, of which waited for: 0 -> 0; matrix products, arithmetic and copies ran while one was open for 22% -> 0% of each run, Pallas kernels for 0% -> 0%
where the time goes in v1:
time: 57.1 us; the launch traced here: 56.5 us
  Pallas kernels  43.7 us (77%)
  local copies, waits for them, and re-layouts  12.1 us (21%)
  between operations  0.66 us (1%)
    pallas_call x1, Pallas kernels, shards(): pl.pallas_call(functools.partial(kernel, tiles, depths), out_shape=(jax.S...  43.7 us
    unnamed x25, local copies, waits for them, and re-layouts  10.7 us
    reshape x1, local copies, waits for them, and re-layouts, shards(): profiles.reshape(4, levels, 1, tiles * cap)  1.41 us

profile of v1, /device:TPU:1, one launch (start us, length us, event | category | flops | bytes accessed | tf_op | source)
XLA Modules:
  0.0 56.5 jit_solution(7694484848191863170)
XLA Ops:
  0.6 0.0 copy-start
  0.6 0.9 %copy-done = f32[4,4,32,128]{3,2,1,0:T(8,128)S(1)} copy-done((f32[4,4,32,128]{3,2,1,0:T(8,128)S(1)}, f32[4,4,32,128]{3,2,1,0:T(8,128)}, u32[]{:S(2)}) %copy-start) | copy-done | bytes 262168
  1.6 0.0 copy-start.1
  1.6 0.9 %copy-done.1 = f32[4,4,32,128]{3,2,1,0:T(8,128)S(1)} copy-done((f32[4,4,32,128]{3,2,1,0:T(8,128)S(1)}, f32[4,4,32,128]{3,2,1,0:T(8,128)}, u32[]{:S(2)}) %copy-start.1) | copy-done | bytes 262168
  2.5 0.0 copy-start.2
  2.5 0.8 %copy-done.2 = f32[4,32,128]{2,1,0:T(8,128)S(1)} copy-done((f32[4,32,128]{2,1,0:T(8,128)S(1)}, f32[4,32,128]{2,1,0:T(8,128)}, u32[]{:S(2)}) %copy-start.2) | copy-done | bytes 65560
  3.4 0.0 copy-start.3
  3.4 0.8 %copy-done.3 = f32[4,32,128]{2,1,0:T(8,128)S(1)} copy-done((f32[4,32,128]{2,1,0:T(8,128)S(1)}, f32[4,32,128]{2,1,0:T(8,128)}, u32[]{:S(2)}) %copy-start.3) | copy-done | bytes 65560
  4.2 0.0 copy-start.4
  4.2 0.8 %copy-done.4 = f32[4,32,128]{2,1,0:T(8,128)S(1)} copy-done((f32[4,32,128]{2,1,0:T(8,128)S(1)}, f32[4,32,128]{2,1,0:T(8,128)}, u32[]{:S(2)}) %copy-start.4) | copy-done | bytes 65560
  5.1 0.0 copy-start.5
  5.1 0.7 %copy-done.5 = s32[32,128]{1,0:T(8,128)S(1)} copy-done((s32[32,128]{1,0:T(8,128)S(1)}, s32[32,128]{1,0:T(8,128)}, u32[]{:S(2)}) %copy-start.5) | copy-done | bytes 16408
  5.8 0.0 copy-start.6
  5.8 0.7 %copy-done.6 = s32[32,128]{1,0:T(8,128)S(1)} copy-done((s32[32,128]{1,0:T(8,128)S(1)}, s32[32,128]{1,0:T(8,128)}, u32[]{:S(2)}) %copy-start.6) | copy-done | bytes 16408
  6.5 0.0 copy-start.7
  6.5 0.7 %copy-done.7 = s32[4096]{0:T(1024)S(1)} copy-done((s32[4096]{0:T(1024)S(1)}, s32[4096]{0:T(1024)}, u32[]{:S(2)}) %copy-start.7) | copy-done | bytes 16408
  7.2 0.0 copy-start.8
  7.2 0.7 %copy-done.8 = s32[4096,1]{0,1:T(1,128)S(1)} copy-done((s32[4096,1]{0,1:T(1,128)S(1)}, s32[4096,1]{0,1:T(1,128)}, u32[]{:S(2)}) %copy-start.8) | copy-done | bytes 16408
  7.9 0.0 copy-start.9
  7.9 0.7 %copy-done.9 = s32[4096]{0:T(1024)S(1)} copy-done((s32[4096]{0:T(1024)S(1)}, s32[4096]{0:T(1024)}, u32[]{:S(2)}) %copy-start.9) | copy-done | bytes 16408
  8.6 0.0 copy-start.10
  8.6 0.7 %copy-done.10 = s32[4096]{0:T(1024)S(1)} copy-done((s32[4096]{0:T(1024)S(1)}, s32[4096]{0:T(1024)}, u32[]{:S(2)}) %copy-start.10) | copy-done | bytes 16408
  9.4 43.7 %shard_map.138 = (f32[4,4,32,128]{3,2,1,0:T(8,128)S(1)}, f32[4,4,32,128]{3,2,1,0:T(8,128)S(1)}, f32[16,8192]{1,0:T(8,128)S(1)}, f32[1,8192]{1,0:T(1,128)S(1)}) custom-call(f32[4,4,32,128]{3,2,1,0:T(8,128)S(1)} %copy-done, f32[4,4,32,128]{3,2,1,0:T(8,128)S(1)} %copy-done.1, s32[32,128]{1,0:T(8,128)S(1)} %copy-done.5, s32[32,128]{1,0:T(8,128)S(1)} %copy-done.6, ...), custom_call_target="tpu_custom_call" | custom-call | tf_op jit(solution)/shard_map/pallas_call | solution.py:641
  53.0 1.4 %reshape.28 = f32[4,4,1,8192]{3,2,1,0:T(1,128)} reshape(f32[16,8192]{1,0:T(8,128)S(1)} %get-tuple-element.10) | data formatting | bytes 1048576 | tf_op jit(solution)/shard_map/reshape | solution.py:709
  54.5 0.7 %copy.19 = f32[4,4,32,128]{3,2,1,0:T(8,128)} copy(f32[4,4,32,128]{3,2,1,0:T(8,128)S(1)} %get-tuple-element.20) | data formatting | bytes 524288
  55.2 0.7 %copy.20 = f32[4,4,32,128]{3,2,1,0:T(8,128)} copy(f32[4,4,32,128]{3,2,1,0:T(8,128)S(1)} %get-tuple-element.21) | data formatting | bytes 524288
  55.9 0.6 %copy.21 = f32[1,8192]{1,0:T(1,128)} copy(f32[1,8192]{1,0:T(1,128)S(1)} %get-tuple-element.23) | data formatting | bytes 65536
Async XLA Ops:
  0.6 1.0 %copy-start = (f32[4,4,32,128]{3,2,1,0:T(8,128)S(1)}, f32[4,4,32,128]{3,2,1,0:T(8,128)}, u32[]{:S(2)}) copy-start(f32[4,4,32,128]{3,2,1,0:T(8,128)} %pert.1) | copy-start | bytes 786436
  1.6 0.9 %copy-start.1 = (f32[4,4,32,128]{3,2,1,0:T(8,128)S(1)}, f32[4,4,32,128]{3,2,1,0:T(8,128)}, u32[]{:S(2)}) copy-start(f32[4,4,32,128]{3,2,1,0:T(8,128)} %cot.1) | copy-start | bytes 786436
  2.5 0.8 %copy-start.2 = (f32[4,32,128]{2,1,0:T(8,128)S(1)}, f32[4,32,128]{2,1,0:T(8,128)}, u32[]{:S(2)}) copy-start(f32[4,32,128]{2,1,0:T(8,128)} %gain.1) | copy-start | bytes 196612
  3.4 0.8 %copy-start.3 = (f32[4,32,128]{2,1,0:T(8,128)S(1)}, f32[4,32,128]{2,1,0:T(8,128)}, u32[]{:S(2)}) copy-start(f32[4,32,128]{2,1,0:T(8,128)} %expan.1) | copy-start | bytes 196612
  4.2 0.8 %copy-start.4 = (f32[4,32,128]{2,1,0:T(8,128)S(1)}, f32[4,32,128]{2,1,0:T(8,128)}, u32[]{:S(2)}) copy-start(f32[4,32,128]{2,1,0:T(8,128)} %contr.1) | copy-start | bytes 196612
  5.1 0.7 %copy-start.5 = (s32[32,128]{1,0:T(8,128)S(1)}, s32[32,128]{1,0:T(8,128)}, u32[]{:S(2)}) copy-start(s32[32,128]{1,0:T(8,128)} %land.1) | copy-start | bytes 49156
  5.8 0.7 %copy-start.6 = (s32[32,128]{1,0:T(8,128)S(1)}, s32[32,128]{1,0:T(8,128)}, u32[]{:S(2)}) copy-start(s32[32,128]{1,0:T(8,128)} %bottom.1) | copy-start | bytes 49156
  6.5 0.7 %copy-start.7 = (s32[4096]{0:T(1024)S(1)}, s32[4096]{0:T(1024)}, u32[]{:S(2)}) copy-start(s32[4096]{0:T(1024)} %param.18) | copy-start | bytes 49156
  7.2 0.7 %copy-start.8 = (s32[4096,1]{0,1:T(1,128)S(1)}, s32[4096,1]{0,1:T(1,128)}, u32[]{:S(2)}) copy-start(s32[4096,1]{0,1:T(1,128)} %param.19) | copy-start | bytes 49156
  7.9 0.7 %copy-start.9 = (s32[4096]{0:T(1024)S(1)}, s32[4096]{0:T(1024)}, u32[]{:S(2)}) copy-start(s32[4096]{0:T(1024)} %param.20) | copy-start | bytes 49156
  8.6 0.7 %copy-start.10 = (s32[4096]{0:T(1024)S(1)}, s32[4096]{0:T(1024)}, u32[]{:S(2)}) copy-start(s32[4096]{0:T(1024)} %param.21) | copy-start | bytes 49156

commit v2 on v1

--- a/solution.py
+++ b/solution.py
@@ -1,4 +1,3 @@
-import functools
 import math
 
 import jax
@@ -10,6 +9,7 @@
 
 STEPS = 2
 LANES = 128
+VMEM_BYTES = 60 * 1024 * 1024
 
 nu_horiz = 0.06
 nu_vert = 0.08
@@ -43,21 +43,16 @@
 def kernel(
     tiles,
     depths,
-    pert,
-    cot,
-    land,
-    bottom,
-    gain,
-    expan,
-    contr,
-    cols,
-    owns,
-    starts,
-    counts,
+    inputs,
+    fin_hbm,
+    adj_hbm,
+    prof_out,
+    sens_out,
+    held,
     fin_out,
     adj_out,
-    prof_out,
-    sens_out,
+    out_sem,
+    load_sem,
     wet,
     gw,
     fin,
@@ -99,8 +94,12 @@
     x_send,
     x_recv,
 ):
+    pert, cot, land, bottom, gain, expan, contr, cols, owns, starts, counts = held
+    loads = [pltpu.make_async_copy(a, b, load_sem.at[i]) for i, (a, b) in enumerate(zip(inputs, held))]
+    for i in (2, 3, 4, 0, 5, 6, 1, 8, 7, 9, 10):
+        loads[i].start()
     levels, rows = wet.shape[0], wet.shape[1]
-    cap = ranks_cap = hot_rank.shape[0]
+    cap = hot_rank.shape[0]
     halves = cap // LANES
     chunks = owns.shape[0]
     planes = 4 * levels
@@ -135,6 +134,8 @@
     lax.fori_loop(1, tiles, greet_tiles, 0)
 
     zero_plane = jnp.zeros((rows, LANES), F32)
+    for copy in loads:
+        copy.wait()
     ocean = land[...] == 1
     for k in range(levels):
         w = jnp.where(ocean & (d * levels + k < bottom[...]), 1.0, 0.0).astype(F32)
@@ -470,6 +471,9 @@
     recv_round(qf, 1, 2, True)
     finish_forward(mid, 1, 2, store_fin)
 
+    keep_fin = pltpu.make_async_copy(fin_out, fin_hbm, out_sem.at[0])
+    keep_fin.start()
+
     groups = planes // 8
     for g in range(groups):
         for r in range(rows):
@@ -526,6 +530,9 @@
     recv_round(qb, 1, 3, False)
     finish_backward(1, 3, store_adj)
 
+    keep_adj = pltpu.make_async_copy(adj_out, adj_hbm, out_sem.at[1])
+    keep_adj.start()
+
     for k in range(levels):
         total = zero_plane
         for f in range(4):
@@ -602,12 +609,39 @@
         return 0
 
     lax.fori_loop(1, depths, drain_exchange, 0)
+    keep_fin.wait()
+    keep_adj.wait()
     own_copy.wait()
     own_sens.wait()
     for buf, sems in ((send_buf, p_sem), (sens_send, s_sem)):
         all_but_one = buf.at[pl.ds(0, tiles - 1)]
         for way in range(2):
             pltpu.make_async_copy(all_but_one, all_but_one, sems.at[way]).wait()
+
+
+def place(fin, adj, sens, prof, fin_out, adj_out, sens_out, prof_out, tiled, lined, sems):
+    planes, width = prof.shape
+    slots = width // LANES
+    groups = planes // 8
+
+    def copy(i, src, dst):
+        made = pltpu.make_async_copy(src, dst, sems.at[i])
+        made.start()
+        return made
+
+    tiles_of = [pl.ds(g * 8, 8) for g in range(groups)]
+    loads = [copy(3 + g, prof.at[at], tiled.at[at]) for g, at in enumerate(tiles_of)]
+    stores = [copy(0, fin, fin_out), copy(1, adj, adj_out), copy(2, sens, sens_out)]
+    for g in range(groups):
+        loads[g].wait()
+        for at in range(slots):
+            lined[pl.ds(g * 8 * slots + at, 8, stride=slots), :] = tiled[
+                g * 8 : g * 8 + 8, at * LANES : (at + 1) * LANES
+            ]
+        part = pl.ds(g * 8 * slots, 8 * slots)
+        stores.append(copy(3 + groups + g, lined.at[part], prof_out.at[part]))
+    for made in stores:
+        made.wait()
 
 
 def shards(
@@ -634,21 +668,41 @@
     def listed(x):
         return x.reshape(chunks, LANES)
 
-    vmem = pl.BlockSpec(memory_space=pltpu.VMEM)
-    hbm = pl.BlockSpec(memory_space=pl.ANY)
+    slots = tiles * cap // LANES
+    operands = (
+        perturbation,
+        cotangent,
+        land_mask,
+        bottom_level,
+        mix_gain,
+        expansion,
+        contraction,
+        listed(columns),
+        listed(owners),
+        listed(level_start),
+        listed(level_count),
+    )
+    hbm = pl.BlockSpec(memory_space=pltpu.HBM)
     state = (4, levels, rows, width)
     dma = pltpu.SemaphoreType.DMA
     final, adjoint, profiles, sensitivity = pl.pallas_call(
-        functools.partial(kernel, tiles, depths),
+        lambda *refs: kernel(
+            tiles, depths, refs[:11], *refs[11:15], refs[18:29], *refs[15:18], *refs[29:]
+        ),
         out_shape=(
             jax.ShapeDtypeStruct(state, F32),
             jax.ShapeDtypeStruct(state, F32),
             jax.ShapeDtypeStruct((planes, tiles * cap), F32),
             jax.ShapeDtypeStruct((1, tiles * cap), F32),
         ),
-        in_specs=[vmem] * 11,
-        out_specs=(vmem, vmem, hbm, hbm),
+        in_specs=[hbm] * 11,
+        out_specs=(hbm,) * 4,
         scratch_shapes=[
+            pltpu.VMEM(state, F32),
+            pltpu.VMEM(state, F32),
+            dma((2,)),
+            *[pltpu.VMEM(x.shape, x.dtype) for x in operands],
+            dma((11,)),
             pltpu.VMEM((levels, rows, width), F32),
             pltpu.VMEM((levels, rows, width), F32),
             pltpu.VMEM((planes * rows, width), F32),
@@ -691,21 +745,26 @@
             dma((depths,)),
         ],
         compiler_params=pltpu.CompilerParams(
-            collective_id=0, has_side_effects=True, vmem_limit_bytes=32 * 1024 * 1024
+            collective_id=0, has_side_effects=True, vmem_limit_bytes=VMEM_BYTES
         ),
-    )(
-        perturbation,
-        cotangent,
-        land_mask,
-        bottom_level,
-        mix_gain,
-        expansion,
-        contraction,
-        listed(columns),
-        listed(owners),
-        listed(level_start),
-        listed(level_count),
-    )
+    )(*operands)
+    final, adjoint, sensitivity, profiles = pl.pallas_call(
+        place,
+        out_shape=(
+            jax.ShapeDtypeStruct(state, F32),
+            jax.ShapeDtypeStruct(state, F32),
+            jax.ShapeDtypeStruct((1, tiles * cap), F32),
+            jax.ShapeDtypeStruct((planes * slots, LANES), F32),
+        ),
+        in_specs=[hbm] * 4,
+        out_specs=(hbm,) * 4,
+        scratch_shapes=[
+            pltpu.VMEM((planes, tiles * cap), F32),
+            pltpu.VMEM((planes * slots, LANES), F32),
+            dma((3 + planes // 4,)),
+        ],
+        compiler_params=pltpu.CompilerParams(vmem_limit_bytes=VMEM_BYTES),
+    )(final, adjoint, sensitivity, profiles)
     return final, adjoint, profiles.reshape(4, levels, 1, tiles * cap), sensitivity
 
 

time: 57.1 us -> 63 us (1.10)
  Pallas kernels: 43.7 us -> 62.2 us
  local copies, waits for them, and re-layouts: 12.1 us -> 0 us
    pallas_call x1 -> x2, Pallas kernels: 43.7 us -> 62.2 us  [the longest x1 44.1 us: shards(): pl.pallas_call(lambda *refs: kernel(tiles, depths, refs[:11], *refs[11:15...]
    unnamed x25 -> x0, local copies, waits for them, and re-layouts: 10.7 us -> none
    reshape x1 -> x0, local copies, waits for them, and re-layouts: 1.41 us -> none  [shards(): profiles.reshape(4, levels, 1, tiles * cap)]
where the time goes in v2:
time: 63 us; the launch traced here: 62.8 us
  Pallas kernels  62.2 us (99%)
  between operations  0.64 us (1%)
    pallas_call x1, Pallas kernels, shards(): pl.pallas_call(lambda *refs: kernel(tiles, depths, refs[:11], *refs[11:15...  44.1 us
    pallas_call x1, Pallas kernels, shards(): pl.pallas_call(place, out_shape=(jax.ShapeDtypeStruct(state, F32), jax.Sh...  18 us

profile of v2, /device:TPU:1, one launch (start us, length us, event | category | flops | bytes accessed | tf_op | source)
XLA Modules:
  0.0 62.8 jit_solution(13083385973658895802)
XLA Ops:
  0.6 44.1 %shard_map.138 = (f32[4,4,32,128]{3,2,1,0:T(8,128)}, f32[4,4,32,128]{3,2,1,0:T(8,128)}, f32[16,8192]{1,0:T(8,128)}, f32[1,8192]{1,0:T(1,128)}) custom-call(f32[4,4,32,128]{3,2,1,0:T(8,128)} %refs_0_.1, f32[4,4,32,128]{3,2,1,0:T(8,128)} %refs_1_.1, s32[32,128]{1,0:T(8,128)} %refs_2_.1, s32[32,128]{1,0:T(8,128)} %refs_3_.1, f32[4,32,128]{2,1,0:T(8,128)} %refs_4_.1, ...), custom_call_target="tpu_custom_call" | custom-call | tf_op jit(solution)/shard_map/pallas_call | solution.py:688
  44.8 18.0 %shard_map.139 = (f32[4,4,32,128]{3,2,1,0:T(8,128)}, f32[4,4,32,128]{3,2,1,0:T(8,128)}, f32[1,8192]{1,0:T(1,128)}, f32[1024,128]{1,0:T(8,128)}) custom-call(f32[4,4,32,128]{3,2,1,0:T(8,128)} %get-tuple-element.12.fin, f32[4,4,32,128]{3,2,1,0:T(8,128)} %get-tuple-element.13.adj, f32[1,8192]{1,0:T(1,128)} %get-tuple-element.14.sens, ...), custom_call_target="tpu_custom_call" | custom-call | tf_op jit(solution)/shard_map/pallas_call | solution.py:751

commit v3 on v2

--- a/solution.py
+++ b/solution.py
@@ -513,20 +513,14 @@
             for g in range(groups):
                 send_buf[owner, g * 8 : g * 8 + 8, h * LANES : (h + 1) * LANES] = totals[g]
 
-        @pl.when(j > 0)
+        @pl.when(j < tiles)
         def _():
             profile_copy(owner).start()
 
         return 0
 
-    lax.fori_loop(0, tiles, gather_owner, 0)
-    own_copy = pltpu.make_async_copy(
-        send_buf.at[t],
-        prof_out.at[:, pl.ds(pl.multiple_of(t * cap, LANES), cap)],
-        x_send.at[0],
-    )
-    own_copy.start()
-
+    first_part, second_part = 1 + tiles * 8 // 32, 1 + tiles * 31 // 32
+    lax.fori_loop(1, first_part, gather_owner, 0)
     recv_round(qb, 1, 3, False)
     finish_backward(1, 3, store_adj)
 
@@ -564,7 +558,7 @@
             sens_part[at, :] = sens_scale * jnp.sum(total, axis=0, keepdims=True)
         return 0
 
-    lax.fori_loop(0, tiles, gather_sens, 0)
+    lax.fori_loop(0, tiles, gather_sens, 0, unroll=4)
 
     def sens_exchange(peer, slot):
         return remote(sens_part, sens_peer.at[slot], x_send.at[1 + peer], x_recv.at[slot], t, peer)
@@ -579,6 +573,7 @@
         return total + sens_peer[peer]
 
     lax.fori_loop(1, depths, start_exchange, 0)
+    lax.fori_loop(first_part, second_part, gather_owner, 0)
     total = lax.fori_loop(1, depths, wait_exchange, sens_part[...])
     for o in range(tiles):
         for h in range(halves):
@@ -598,6 +593,14 @@
     lax.fori_loop(1, tiles, start_sens, 0)
     own_sens = pltpu.make_async_copy(sens_send.at[t], sens_out.at[:, mine], x_recv.at[d])
     own_sens.start()
+    lax.fori_loop(second_part, tiles + 1, gather_owner, 0)
+    own_copy = pltpu.make_async_copy(
+        send_buf.at[t],
+        prof_out.at[:, pl.ds(pl.multiple_of(t * cap, LANES), cap)],
+        x_send.at[0],
+    )
+    own_copy.start()
+
 
     drain_round(qf, 0, 0, True)
     drain_round(qb, 0, 1, False)
@@ -619,7 +622,8 @@
             pltpu.make_async_copy(all_but_one, all_but_one, sems.at[way]).wait()
 
 
-def place(fin, adj, sens, prof, fin_out, adj_out, sens_out, prof_out, tiled, lined, sems):
+def place(fin, adj, sens, prof, fin_out, adj_out, sens_out, prof_out, *scratch):
+    fin_held, adj_held, sens_held, tiled, lined, sems = scratch
     planes, width = prof.shape
     slots = width // LANES
     groups = planes // 8
@@ -629,9 +633,15 @@
         made.start()
         return made
 
-    tiles_of = [pl.ds(g * 8, 8) for g in range(groups)]
-    loads = [copy(3 + g, prof.at[at], tiled.at[at]) for g, at in enumerate(tiles_of)]
-    stores = [copy(0, fin, fin_out), copy(1, adj, adj_out), copy(2, sens, sens_out)]
+    loads = [
+        copy(g, prof.at[pl.ds(g * 8, 8)], tiled.at[pl.ds(g * 8, 8)]) for g in range(groups)
+    ]
+    passed = ((fin, fin_held, fin_out), (adj, adj_held, adj_out), (sens, sens_held, sens_out))
+    loads += [copy(groups + i, src, held) for i, (src, held, _) in enumerate(passed)]
+    stores = []
+    for i, (_, held, out) in enumerate(passed):
+        loads[groups + i].wait()
+        stores.append(copy(groups + 3 + i, held, out))
     for g in range(groups):
         loads[g].wait()
         for at in range(slots):
@@ -639,7 +649,7 @@
                 g * 8 : g * 8 + 8, at * LANES : (at + 1) * LANES
             ]
         part = pl.ds(g * 8 * slots, 8 * slots)
-        stores.append(copy(3 + groups + g, lined.at[part], prof_out.at[part]))
+        stores.append(copy(groups + 6 + g, lined.at[part], prof_out.at[part]))
     for made in stores:
         made.wait()
 
@@ -759,9 +769,12 @@
         in_specs=[hbm] * 4,
         out_specs=(hbm,) * 4,
         scratch_shapes=[
+            pltpu.VMEM(state, F32),
+            pltpu.VMEM(state, F32),
+            pltpu.VMEM((1, tiles * cap), F32),
             pltpu.VMEM((planes, tiles * cap), F32),
             pltpu.VMEM((planes * slots, LANES), F32),
-            dma((3 + planes // 4,)),
+            dma((6 + planes // 4,)),
         ],
         compiler_params=pltpu.CompilerParams(vmem_limit_bytes=VMEM_BYTES),
     )(final, adjoint, sensitivity, profiles)

time: 63 us -> 42.6 us (0.68)
  Pallas kernels: 62.2 us -> 41.9 us
    pallas_call x1, Pallas kernels: 18 us -> 2.3 us  [shards(): pl.pallas_call(place, out_shape=(jax.ShapeDtypeStruct(state, F32), jax.Sh...]
    pallas_call x1, Pallas kernels: 44.1 us -> 39.6 us  [shards(): pl.pallas_call(lambda *refs: kernel(tiles, depths, refs[:11], *refs[11:15...]
where the time goes in v3:
time: 42.6 us; the launch traced here: 42.5 us
  Pallas kernels  41.9 us (98%)
  between operations  0.64 us (2%)
    pallas_call x1, Pallas kernels, shards(): pl.pallas_call(lambda *refs: kernel(tiles, depths, refs[:11], *refs[11:15...  39.6 us
    pallas_call x1, Pallas kernels, shards(): pl.pallas_call(place, out_shape=(jax.ShapeDtypeStruct(state, F32), jax.Sh...  2.3 us

profile of v3, /device:TPU:1, one launch (start us, length us, event | category | flops | bytes accessed | tf_op | source)
XLA Modules:
  0.0 42.5 jit_solution(16180506337247600351)
XLA Ops:
  0.6 39.6 %shard_map.138 = (f32[4,4,32,128]{3,2,1,0:T(8,128)}, f32[4,4,32,128]{3,2,1,0:T(8,128)}, f32[16,8192]{1,0:T(8,128)}, f32[1,8192]{1,0:T(1,128)}) custom-call(f32[4,4,32,128]{3,2,1,0:T(8,128)} %refs_0_.1, f32[4,4,32,128]{3,2,1,0:T(8,128)} %refs_1_.1, s32[32,128]{1,0:T(8,128)} %refs_2_.1, s32[32,128]{1,0:T(8,128)} %refs_3_.1, f32[4,32,128]{2,1,0:T(8,128)} %refs_4_.1, ...), custom_call_target="tpu_custom_call" | custom-call | tf_op jit(solution)/shard_map/pallas_call | solution.py:698
  40.2 2.3 %shard_map.139 = (f32[4,4,32,128]{3,2,1,0:T(8,128)}, f32[4,4,32,128]{3,2,1,0:T(8,128)}, f32[1,8192]{1,0:T(1,128)}, f32[1024,128]{1,0:T(8,128)}) custom-call(f32[4,4,32,128]{3,2,1,0:T(8,128)} %get-tuple-element.12.fin, f32[4,4,32,128]{3,2,1,0:T(8,128)} %get-tuple-element.13.adj, f32[1,8192]{1,0:T(1,128)} %get-tuple-element.14.sens, ...), custom_call_target="tpu_custom_call" | custom-call | tf_op jit(solution)/shard_map/pallas_call | solution.py:761

commit v4 on v3

--- a/solution.py
+++ b/solution.py
@@ -134,8 +134,12 @@
     lax.fori_loop(1, tiles, greet_tiles, 0)
 
     zero_plane = jnp.zeros((rows, LANES), F32)
-    for copy in loads:
-        copy.wait()
+
+    def loaded(*which):
+        for i in which:
+            loads[i].wait()
+
+    loaded(2, 3, 4, 0, 5, 6)
     ocean = land[...] == 1
     for k in range(levels):
         w = jnp.where(ocean & (d * levels + k < bottom[...]), 1.0, 0.0).astype(F32)
@@ -222,19 +226,19 @@
 
     def level_up(q, s, rnd):
         return remote(
-            q.at[s, :, levels], q.at[s, :, 0], q_send.at[rnd, 1], q_recv.at[rnd, 0], t, d + 1
+            q.at[s, :, levels], q.at[s, :, 0], q_send.at[1], q_recv.at[rnd, 0], t, d + 1
         )
 
     def level_down(q, s, rnd):
         return remote(
-            q.at[s, :, 1], q.at[s, :, levels + 1], q_send.at[rnd, 0], q_recv.at[rnd, 1], t, d - 1
+            q.at[s, :, 1], q.at[s, :, levels + 1], q_send.at[0], q_recv.at[rnd, 1], t, d - 1
         )
 
     def edge_copy(rnd, side):
         return remote(
             edge_out.at[rnd, side],
             edge_in.at[rnd, 1 - side],
-            e_send.at[rnd, side],
+            e_send.at[side],
             e_recv.at[rnd, 1 - side],
             t - 1 if side == 0 else t + 1,
             d,
@@ -242,14 +246,14 @@
 
     def tot_copy(rnd, peer, slot):
         return remote(
-            tot_out.at[rnd], tot_in.at[rnd, slot], t_send.at[rnd, peer], t_recv.at[rnd, slot], t, peer
+            tot_out.at[rnd], tot_in.at[rnd, slot], t_send.at[0], t_recv.at[rnd, slot], t, peer
         )
 
     def diag_copy(rnd, side, peer, slot):
         return remote(
             diag_out.at[rnd, side],
             diag_in.at[rnd, 1 - side, slot],
-            d_send.at[rnd, side, peer],
+            d_send.at[side],
             d_recv.at[rnd, 1 - side, slot],
             t - 1 if side == 0 else t + 1,
             peer,
@@ -316,31 +320,24 @@
         def _():
             level_down(q, s, rnd).wait_recv()
 
-    def drain_round(q, s, rnd, forward):
-        def one(peer, _):
-            tot_copy(rnd, peer, d).wait_send()
-            for side in range(2):
-
-                @pl.when(has_side[side])
-                def _():
-                    diag_copy(rnd, side, peer, d).wait_send()
-
-            return 0
-
-        lax.fori_loop(*ahead(forward), one, 0)
+    def drain(part, sem):
+        pltpu.make_async_copy(part, part, sem).wait()
+
+    def drain_rounds():
+        others = pl.ds(0, depths - 1)
+        drain(tot_in.at[pl.ds(0, 2), others], t_send.at[0])
         for side in range(2):
 
             @pl.when(has_side[side])
             def _():
-                edge_copy(rnd, side).wait_send()
-
-        @pl.when(d < depths - 1)
-        def _():
-            level_up(q, s, rnd).wait_send()
-
-        @pl.when(d > 0)
-        def _():
-            level_down(q, s, rnd).wait_send()
+                drain(edge_in.at[:, side], e_send.at[side])
+                drain(diag_in.at[pl.ds(0, 2), side, others], d_send.at[side])
+
+        for way, there in ((0, d > 0), (1, d < depths - 1)):
+
+            @pl.when(there)
+            def _():
+                drain(qf.at[0, :, pl.ds(1, 4)], q_send.at[way])
 
     def base_sums(rnd, forward):
         def one(peer, carry):
@@ -399,13 +396,15 @@
             store(3, k, a_v + mixed(qb, s, rnd, 3, k) + coriolis * a_u)
 
     prepare_forward(pert, 0, 0)
-    prepare_backward(cot, 0, 1)
 
     sides = has_side[0].astype(I32) + has_side[1].astype(I32)
     pl.semaphore_wait(barrier, (depths - 1) * (1 + sides) + tiles - 1)
 
     send_round(qf, 0, 0, True)
+    loaded(1)
+    prepare_backward(cot, 0, 1)
     send_round(qb, 0, 1, False)
+    loaded(8, 7, 9, 10)
 
     own_ids = iota((tiles, LANES), 0)
 
@@ -519,7 +518,7 @@
 
         return 0
 
-    first_part, second_part = 1 + tiles * 8 // 32, 1 + tiles * 31 // 32
+    first_part, second_part = 1 + tiles * 16 // 32, 1 + tiles * 31 // 32
     lax.fori_loop(1, first_part, gather_owner, 0)
     recv_round(qb, 1, 3, False)
     finish_backward(1, 3, store_adj)
@@ -561,7 +560,7 @@
     lax.fori_loop(0, tiles, gather_sens, 0, unroll=4)
 
     def sens_exchange(peer, slot):
-        return remote(sens_part, sens_peer.at[slot], x_send.at[1 + peer], x_recv.at[slot], t, peer)
+        return remote(sens_part, sens_peer.at[slot], x_send.at[1], x_recv.at[slot], t, peer)
 
     def start_exchange(j, _):
         sens_exchange(lax.rem(d + j, depths), d).start()
@@ -602,16 +601,9 @@
     own_copy.start()
 
 
-    drain_round(qf, 0, 0, True)
-    drain_round(qb, 0, 1, False)
-    drain_round(qf, 1, 2, True)
-    drain_round(qb, 1, 3, False)
-
-    def drain_exchange(j, _):
-        sens_exchange(lax.rem(d + j, depths), d).wait_send()
-        return 0
-
-    lax.fori_loop(1, depths, drain_exchange, 0)
+    drain_rounds()
+
+    drain(sens_peer.at[pl.ds(0, depths - 1)], x_send.at[1])
     keep_fin.wait()
     keep_adj.wait()
     own_copy.wait()
@@ -741,17 +733,17 @@
             pltpu.VMEM((cap // LANES * tiles, LANES), F32),
             pltpu.VMEM((depths, cap // LANES * tiles, LANES), F32),
             pltpu.VMEM((tiles, 1, cap), F32),
+            dma((2,)),
             dma((4, 2)),
+            dma((2,)),
             dma((4, 2)),
-            dma((4, 2)),
-            dma((4, 2)),
+            dma((1,)),
             dma((4, depths)),
-            dma((4, depths)),
-            dma((4, 2, depths)),
+            dma((2,)),
             dma((4, 2, depths)),
             dma((2,)),
             dma((2,)),
-            dma((1 + depths,)),
+            dma((2,)),
             dma((depths,)),
         ],
         compiler_params=pltpu.CompilerParams(

time: 42.6 us -> 41.4 us (0.972)
  Pallas kernels: 41.9 us -> 40.6 us
    pallas_call x1, Pallas kernels: 39.6 us -> 38.3 us  [shards(): pl.pallas_call(lambda *refs: kernel(tiles, depths, refs[:11], *refs[11:15...]
where the time goes in v4:
time: 41.4 us; the launch traced here: 41.2 us
  Pallas kernels  40.6 us (98%)
  between operations  0.64 us (2%)
    pallas_call x1, Pallas kernels, shards(): pl.pallas_call(lambda *refs: kernel(tiles, depths, refs[:11], *refs[11:15...  38.3 us
    pallas_call x1, Pallas kernels, shards(): pl.pallas_call(place, out_shape=(jax.ShapeDtypeStruct(state, F32), jax.Sh...  2.3 us

profile of v4, /device:TPU:1, one launch (start us, length us, event | category | flops | bytes accessed | tf_op | source)
XLA Modules:
  0.0 41.2 jit_solution(169958099308017375)
XLA Ops:
  0.6 38.3 %shard_map.138 = (f32[4,4,32,128]{3,2,1,0:T(8,128)}, f32[4,4,32,128]{3,2,1,0:T(8,128)}, f32[16,8192]{1,0:T(8,128)}, f32[1,8192]{1,0:T(1,128)}) custom-call(f32[4,4,32,128]{3,2,1,0:T(8,128)} %refs_0_.1, f32[4,4,32,128]{3,2,1,0:T(8,128)} %refs_1_.1, s32[32,128]{1,0:T(8,128)} %refs_2_.1, s32[32,128]{1,0:T(8,128)} %refs_3_.1, f32[4,32,128]{2,1,0:T(8,128)} %refs_4_.1, ...), custom_call_target="tpu_custom_call" | custom-call | tf_op jit(solution)/shard_map/pallas_call | solution.py:690
  38.9 2.3 %shard_map.139 = (f32[4,4,32,128]{3,2,1,0:T(8,128)}, f32[4,4,32,128]{3,2,1,0:T(8,128)}, f32[1,8192]{1,0:T(1,128)}, f32[1024,128]{1,0:T(8,128)}) custom-call(f32[4,4,32,128]{3,2,1,0:T(8,128)} %get-tuple-element.12.fin, f32[4,4,32,128]{3,2,1,0:T(8,128)} %get-tuple-element.13.adj, f32[1,8192]{1,0:T(1,128)} %get-tuple-element.14.sens, ...), custom_call_target="tpu_custom_call" | custom-call | tf_op jit(solution)/shard_map/pallas_call | solution.py:753

commit v5 on v4

--- a/solution.py
+++ b/solution.py
@@ -93,6 +93,7 @@
     s_sem,
     x_send,
     x_recv,
+    ready,
 ):
     pert, cot, land, bottom, gain, expan, contr, cols, owns, starts, counts = held
     loads = [pltpu.make_async_copy(a, b, load_sem.at[i]) for i, (a, b) in enumerate(zip(inputs, held))]
@@ -127,11 +128,32 @@
 
     lax.fori_loop(1, depths, greet_depths, 0)
 
-    def greet_tiles(j, _):
-        greet(lax.rem(t + j, tiles), d)
+    for side, there in ((t - 1, t > 0), (t + 1, t < tiles - 1)):
+
+        @pl.when(there)
+        def _():
+            greet(side, d)
+
+    across = 8 if tiles % 8 == 0 else 2
+    down = tiles // across
+    my_row, my_col = t // across, lax.rem(t, across)
+
+    def in_column(j):
+        return lax.rem(my_row + j, down) * across + my_col
+
+    def in_row(j):
+        return my_row * across + lax.rem(my_col + j, across)
+
+    def greet_column(j, _):
+        greet(in_column(j), d)
         return 0
 
-    lax.fori_loop(1, tiles, greet_tiles, 0)
+    def greet_row(j, _):
+        greet(in_row(j), d)
+        return 0
+
+    lax.fori_loop(1, down, greet_column, 0)
+    lax.fori_loop(1, across, greet_row, 0)
 
     zero_plane = jnp.zeros((rows, LANES), F32)
 
@@ -398,13 +420,19 @@
     prepare_forward(pert, 0, 0)
 
     sides = has_side[0].astype(I32) + has_side[1].astype(I32)
-    pl.semaphore_wait(barrier, (depths - 1) * (1 + sides) + tiles - 1)
+    pl.semaphore_wait(barrier, (depths - 1) * (1 + sides) + sides + down + across - 2)
 
     send_round(qf, 0, 0, True)
     loaded(1)
     prepare_backward(cot, 0, 1)
     send_round(qb, 0, 1, False)
     loaded(8, 7, 9, 10)
+
+    def vouch(j, _):
+        pl.semaphore_signal(ready, inc=1, device_id=(in_row(j), d), device_id_type=MESH)
+        return 0
+
+    lax.fori_loop(1, across, vouch, 0)
 
     own_ids = iota((tiles, LANES), 0)
 
@@ -519,6 +547,7 @@
         return 0
 
     first_part, second_part = 1 + tiles * 16 // 32, 1 + tiles * 31 // 32
+    pl.semaphore_wait(ready, across - 1)
     lax.fori_loop(1, first_part, gather_owner, 0)
     recv_round(qb, 1, 3, False)
     finish_backward(1, 3, store_adj)
@@ -745,6 +774,7 @@
             dma((2,)),
             dma((2,)),
             dma((depths,)),
+            pltpu.SemaphoreType.REGULAR,
         ],
         compiler_params=pltpu.CompilerParams(
             collective_id=0, has_side_effects=True, vmem_limit_bytes=VMEM_BYTES

time: 41.4 us -> 41.2 us (level)
  no operation moved by 1% of the time
where the time goes in v5:
time: 41.2 us; the launch traced here: 41 us
  Pallas kernels  40.3 us (98%)
  between operations  0.64 us (2%)
    pallas_call x1, Pallas kernels, shards(): pl.pallas_call(lambda *refs: kernel(tiles, depths, refs[:11], *refs[11:15...  38 us
    pallas_call x1, Pallas kernels, shards(): pl.pallas_call(place, out_shape=(jax.ShapeDtypeStruct(state, F32), jax.Sh...  2.3 us

profile of v5, /device:TPU:1, one launch (start us, length us, event | category | flops | bytes accessed | tf_op | source)
XLA Modules:
  0.0 41.0 jit_solution(1974254811274181137)
XLA Ops:
  0.6 38.0 %shard_map.138 = (f32[4,4,32,128]{3,2,1,0:T(8,128)}, f32[4,4,32,128]{3,2,1,0:T(8,128)}, f32[16,8192]{1,0:T(8,128)}, f32[1,8192]{1,0:T(1,128)}) custom-call(f32[4,4,32,128]{3,2,1,0:T(8,128)} %refs_0_.1, f32[4,4,32,128]{3,2,1,0:T(8,128)} %refs_1_.1, s32[32,128]{1,0:T(8,128)} %refs_2_.1, s32[32,128]{1,0:T(8,128)} %refs_3_.1, f32[4,32,128]{2,1,0:T(8,128)} %refs_4_.1, ...), custom_call_target="tpu_custom_call" | custom-call | tf_op jit(solution)/shard_map/pallas_call | solution.py:719
  38.7 2.3 %shard_map.139 = (f32[4,4,32,128]{3,2,1,0:T(8,128)}, f32[4,4,32,128]{3,2,1,0:T(8,128)}, f32[1,8192]{1,0:T(1,128)}, f32[1024,128]{1,0:T(8,128)}) custom-call(f32[4,4,32,128]{3,2,1,0:T(8,128)} %get-tuple-element.12.fin, f32[4,4,32,128]{3,2,1,0:T(8,128)} %get-tuple-element.13.adj, f32[1,8192]{1,0:T(1,128)} %get-tuple-element.14.sens, ...), custom_call_target="tpu_custom_call" | custom-call | tf_op jit(solution)/shard_map/pallas_call | solution.py:783
